TPU v7x, 32 devices: a whole 2x2x4 slice. The times are simulated.
32 devices in a mesh: narrow: 8 (over z, y), wide: 4 (over x, core).
Axes of the slice: x: 2, y: 2, z: 4, core: 2. Of those that a mesh axis runs over, the one named last changes fastest.
Arguments:
- tokens: bfloat16 [2048, 2, 2048], P(('narrow', 'wide')), may hold values from -6 to 6
- lengths: int32 [2], replicated, may hold values from 64 to 2048, as said below
- attn_gain: float32 [2048], replicated, may hold values from 0.1 to 1.9
- w_query: bfloat16 [2048, 2048], P(None, 'wide'), may hold values from -0.125 to 0.125
- key_matrix: bfloat16 [2048, 512], P(None, 'wide'), may hold values from -0.125 to 0.125
- value_matrix: bfloat16 [2048, 512], P(None, 'wide'), may hold values from -0.125 to 0.125
- q_gain: float32 [64], replicated, may hold values from 0.1 to 1.9
- k_gain: float32 [64], replicated, may hold values from 0.1 to 1.9
- w_out: bfloat16 [2048, 2048], P('wide'), may hold values from -1 to 1
- ffn_gain: float32 [2048], replicated, may hold values from 0.1 to 1.9
- w_gate: bfloat16 [2048, 8192], P(None, 'wide'), may hold values from -0.125 to 0.125
- w_up: bfloat16 [2048, 8192], P(None, 'wide'), may hold values from -0.125 to 0.125
- w_down: bfloat16 [8192, 2048], P('wide'), may hold values from -0.0625 to 0.0625
- out_grad: bfloat16 [2048, 2, 2048], P(('narrow', 'wide')), may hold values from -6 to 6
Outputs:
- mixed: bfloat16 [2048, 2, 2048], P(('narrow', 'wide'))
- d_tokens: float32 [2048, 2, 2048], P(('narrow', 'wide'))
- d_attn_gain: float32 [2048], replicated
- d_w_query: float32 [2048, 2048], P('narrow', 'wide')
- d_w_key: float32 [2048, 512], P('narrow', 'wide')
- d_w_value: float32 [2048, 512], P('narrow', 'wide')
- d_q_gain: float32 [64], replicated
- d_k_gain: float32 [64], replicated
- d_w_out_t: float32 [2048, 2048], P('narrow', 'wide')
- d_ffn_gain: float32 [2048], replicated
- d_w_gate: float32 [2048, 8192], P('narrow', 'wide')
- d_w_up: float32 [2048, 8192], P('narrow', 'wide')
- d_w_down_t: float32 [2048, 8192], P('narrow', 'wide')
Inputs may be any that keep to these rules, and one draw needn't show every extreme that they name: `lengths`: in every draw one row, drawn from the seed, uses all 2048 slots; the others are mostly short.
All inputs are finite; a program needn't handle non-finite values.
Results may differ from a plain program's by a relative error of at most 0.02.
Values may be sent and summed in bfloat16 or wider, within the bound.
No kernel may reach another device: no remote copies, remote signals or barrier semaphores. Data moves between devices by JAX's collectives and lax.ppermute only.
A program may use at most 256 MiB of HBM per device.

v0:
```python
import math

import jax
import jax.numpy as jnp
from jax import lax
from jax.sharding import PartitionSpec as P

QUERY_HEADS = 32
KEY_VALUE_HEADS = 8
HEAD_WIDTH = 64


EPS = 1e-06
NEG = -1e30


def rows_normalize(value_rows, gain):
    return (
        value_rows
        * lax.rsqrt(jnp.mean(value_rows * value_rows, axis=-1, keepdims=True) + EPS)
        * gain
    )


def row_norm_back(value_rows, gain, grad):
    _, pull = jax.vjp(rows_normalize, value_rows, gain)
    return pull(grad)


def rotary_tables(positions, head_size):
    half = head_size // 2
    freqs = jnp.exp(-math.log(10000.0) * jnp.arange(half, dtype=jnp.float32) * 2.0 / head_size)
    angles = positions.astype(jnp.float32)[:, None] * freqs[None, :]
    return (jnp.cos(angles), jnp.sin(angles))


def rotary_apply(value_rows, cosine_table, sine_table):
    half = value_rows.shape[-1] // 2
    first = value_rows[..., :half]
    second = value_rows[..., half:]
    cos_b = cosine_table[:, None, None, :]
    sin_b = sine_table[:, None, None, :]
    return jnp.concatenate(
        [first * cos_b - second * sin_b, second * cos_b + first * sin_b], axis=-1
    )


def swiglu(gate, up):
    return jax.nn.silu(gate) * up


def inner_rows(left, right):
    return lax.dot_general(
        left, right, (((0,), (0,)), ((), ())), preferred_element_type=jnp.float32
    )


def times_transposed(left, right):
    return lax.dot_general(
        left, right, (((1,), (1,)), ((), ())), preferred_element_type=jnp.float32
    )


def head_scores(query_h, key_h, allowed, scale):
    scores = jnp.einsum("qsd,ksd->sqk", query_h, key_h, preferred_element_type=jnp.float32) * scale
    return jnp.where(allowed, scores, NEG)


def shards(
    tokens,
    lengths,
    attn_gain,
    w_query,
    key_matrix,
    value_matrix,
    q_gain,
    k_gain,
    w_out,
    ffn_gain,
    w_gate,
    w_up,
    w_down,
    out_grad,
):
    wide_count = lax.axis_size("wide")
    wide_index = lax.axis_index("wide")
    narrow_index = lax.axis_index("narrow")
    share, seqs, width = tokens.shape
    stretch = share * wide_count
    rows = stretch * seqs
    share_rows = share * seqs
    head_size = HEAD_WIDTH
    local_heads = w_query.shape[1] // head_size
    kv_local = key_matrix.shape[1] // head_size
    query_group = QUERY_HEADS // KEY_VALUE_HEADS
    scale = head_size ** (-0.5)
    positions = narrow_index * stretch + jnp.arange(stretch, dtype=jnp.int32)
    share_positions = (
        narrow_index * stretch + wide_index * share + jnp.arange(share, dtype=jnp.int32)
    )
    whole = lax.all_gather(tokens, "wide", axis=0, tiled=True)
    resid = whole.astype(jnp.float32).reshape(rows, width)
    normed = rows_normalize(resid, attn_gain).astype(jnp.bfloat16)
    query_raw = jnp.dot(normed, w_query, preferred_element_type=jnp.float32).reshape(
        stretch, seqs, local_heads, head_size
    )
    key_unnormed = jnp.dot(normed, key_matrix, preferred_element_type=jnp.float32).reshape(
        stretch, seqs, kv_local, head_size
    )
    value_unnormed = jnp.dot(normed, value_matrix, preferred_element_type=jnp.float32)
    cosine_table, sine_table = rotary_tables(positions, head_size)
    query = rotary_apply(rows_normalize(query_raw, q_gain), cosine_table, sine_table).astype(
        jnp.bfloat16
    )
    key_rows = rotary_apply(rows_normalize(key_unnormed, k_gain), cosine_table, sine_table).astype(
        jnp.bfloat16
    )
    value_rows = value_unnormed.reshape(stretch, seqs, kv_local, head_size).astype(jnp.bfloat16)
    all_keys, all_values = (
        lax.all_gather(key_rows, "narrow", axis=0, tiled=True),
        lax.all_gather(value_rows, "narrow", axis=0, tiled=True),
    )
    key_count = all_keys.shape[0]
    key_positions = jnp.arange(key_count, dtype=jnp.int32)
    allowed = (key_positions[None, None, :] <= positions[None, :, None]) & (
        key_positions[None, None, :] < lengths[:, None, None]
    )
    head_pick = jnp.arange(local_heads, dtype=jnp.int32) // query_group
    query_heads = jnp.moveaxis(query, 2, 0)

    def head_forward(item):
        query_h, pick = item
        key_h = lax.dynamic_index_in_dim(all_keys, pick, 2, keepdims=False)
        value_h = lax.dynamic_index_in_dim(all_values, pick, 2, keepdims=False)
        scores = head_scores(query_h, key_h, allowed, scale)
        peak = jnp.max(scores, axis=-1, keepdims=True)
        expo = jnp.exp(scores - peak)
        total = jnp.sum(expo, axis=-1, keepdims=True)
        probs = (expo / total).astype(jnp.bfloat16)
        mixed_h = jnp.einsum("sqk,ksd->qsd", probs, value_h, preferred_element_type=jnp.float32)
        return (mixed_h.astype(jnp.bfloat16), (peak + jnp.log(total))[..., 0])

    mixed_heads, log_totals = lax.map(head_forward, (query_heads, head_pick))
    heads_out = jnp.moveaxis(mixed_heads, 0, 2).reshape(rows, local_heads * head_size)
    attn_part = jnp.dot(heads_out, w_out, preferred_element_type=jnp.float32)
    attn = lax.psum(attn_part.astype(jnp.bfloat16), "wide").astype(jnp.float32)
    resid_mid = resid + attn
    mid_normed = rows_normalize(resid_mid, ffn_gain).astype(jnp.bfloat16)
    mid_share = lax.dynamic_slice_in_dim(resid_mid, wide_index * share_rows, share_rows, 0)
    gate = jnp.dot(mid_normed, w_gate, preferred_element_type=jnp.float32)
    up = jnp.dot(mid_normed, w_up, preferred_element_type=jnp.float32)
    hidden = swiglu(gate, up).astype(jnp.bfloat16)
    ffn_share = lax.psum_scatter(
        jnp.dot(hidden, w_down, preferred_element_type=jnp.float32).astype(jnp.bfloat16),
        "wide",
        scatter_dimension=0,
        tiled=True,
    ).astype(jnp.float32)
    output = (mid_share + ffn_share).reshape(share, seqs, width).astype(jnp.bfloat16)
    share_valid = share_positions[:, None] < lengths[None, :]
    grad_share = jnp.where(share_valid[:, :, None], out_grad, jnp.zeros_like(out_grad))
    grad_whole = lax.all_gather(grad_share, "wide", axis=0, tiled=True).reshape(rows, width)
    hidden_grad = times_transposed(grad_whole, w_down)
    d_down_t = inner_rows(grad_whole, hidden)
    _, pull_glu = jax.vjp(swiglu, gate, up)
    gate_grad, up_grad = pull_glu(hidden_grad)
    gate_grad = gate_grad.astype(jnp.bfloat16)
    up_grad = up_grad.astype(jnp.bfloat16)
    d_gate = inner_rows(mid_normed, gate_grad)
    d_up = inner_rows(mid_normed, up_grad)
    normed_grad = times_transposed(gate_grad, w_gate) + times_transposed(up_grad, w_up)
    mid_part, ffn_gain_grad = row_norm_back(resid_mid, ffn_gain, normed_grad)
    mid_grad = grad_whole.astype(jnp.float32) + lax.psum(
        mid_part.astype(jnp.bfloat16), "wide"
    ).astype(jnp.float32)
    mid_grad_share = lax.dynamic_slice_in_dim(mid_grad, wide_index * share_rows, share_rows, 0)
    mid_low = mid_grad.astype(jnp.bfloat16)
    d_out_t = inner_rows(mid_low, heads_out)
    heads_grad = times_transposed(mid_low, w_out).astype(jnp.bfloat16)
    grad_heads = jnp.moveaxis(heads_grad.reshape(stretch, seqs, local_heads, head_size), 2, 0)

    def head_backward(carry, item):
        key_acc, value_acc = carry
        query_h, grad_h, log_h, pick = item
        key_h = lax.dynamic_index_in_dim(all_keys, pick, 2, keepdims=False)
        value_h = lax.dynamic_index_in_dim(all_values, pick, 2, keepdims=False)
        scores = head_scores(query_h, key_h, allowed, scale)
        probs = jnp.where(allowed, jnp.exp(scores - log_h[..., None]), 0.0)
        value_grad = jnp.einsum(
            "sqk,qsd->ksd", probs.astype(jnp.bfloat16), grad_h, preferred_element_type=jnp.float32
        )
        prob_grad = jnp.einsum("qsd,ksd->sqk", grad_h, value_h, preferred_element_type=jnp.float32)
        inner = jnp.sum(probs * prob_grad, axis=-1, keepdims=True)
        score_grad = (probs * (prob_grad - inner)).astype(jnp.bfloat16)
        query_grad = (
            jnp.einsum("sqk,ksd->qsd", score_grad, key_h, preferred_element_type=jnp.float32)
            * scale
        )
        key_grad = (
            jnp.einsum("sqk,qsd->ksd", score_grad, query_h, preferred_element_type=jnp.float32)
            * scale
        )
        key_acc = lax.dynamic_update_index_in_dim(
            key_acc, lax.dynamic_index_in_dim(key_acc, pick, 2, keepdims=False) + key_grad, pick, 2
        )
        value_acc = lax.dynamic_update_index_in_dim(
            value_acc,
            lax.dynamic_index_in_dim(value_acc, pick, 2, keepdims=False) + value_grad,
            pick,
            2,
        )
        return ((key_acc, value_acc), query_grad)

    empty = jnp.zeros(all_keys.shape, jnp.float32)
    (key_grad_all, value_grad_all), query_grads = lax.scan(
        head_backward, (empty, empty), (query_heads, grad_heads, log_totals, head_pick)
    )
    key_grad, value_grad = (
        lax.psum_scatter(
            key_grad_all.astype(jnp.bfloat16), "narrow", scatter_dimension=0, tiled=True
        ).astype(jnp.float32),
        lax.psum_scatter(
            value_grad_all.astype(jnp.bfloat16), "narrow", scatter_dimension=0, tiled=True
        ).astype(jnp.float32),
    )
    query_grad = rotary_apply(jnp.moveaxis(query_grads, 0, 2), cosine_table, -sine_table)
    query_pre, q_gain_grad = row_norm_back(query_raw, q_gain, query_grad)
    key_pre, k_gain_grad = row_norm_back(
        key_unnormed, k_gain, rotary_apply(key_grad, cosine_table, -sine_table)
    )
    query_raw_grad = query_pre.reshape(rows, local_heads * head_size).astype(jnp.bfloat16)
    key_raw_grad = key_pre.reshape(rows, kv_local * head_size).astype(jnp.bfloat16)
    value_raw_grad = value_grad.reshape(rows, kv_local * head_size).astype(jnp.bfloat16)
    d_query = inner_rows(normed, query_raw_grad)
    d_key = inner_rows(normed, key_raw_grad)
    d_value = inner_rows(normed, value_raw_grad)
    normed_grad_attn = (
        times_transposed(query_raw_grad, w_query)
        + times_transposed(key_raw_grad, key_matrix)
        + times_transposed(value_raw_grad, value_matrix)
    )
    token_part, attn_gain_grad = row_norm_back(resid, attn_gain, normed_grad_attn)
    token_share = lax.psum_scatter(
        token_part.astype(jnp.bfloat16), "wide", scatter_dimension=0, tiled=True
    ).astype(jnp.float32)
    d_tokens = (mid_grad_share + token_share).reshape(share, seqs, width)
    d_query_s, d_key_s, d_value_s, d_gate_s, d_up_s, d_out_s, d_down_s = (
        lax.psum_scatter(
            d_query.astype(jnp.bfloat16), "narrow", scatter_dimension=0, tiled=True
        ).astype(jnp.float32),
        lax.psum_scatter(
            d_key.astype(jnp.bfloat16), "narrow", scatter_dimension=0, tiled=True
        ).astype(jnp.float32),
        lax.psum_scatter(
            d_value.astype(jnp.bfloat16), "narrow", scatter_dimension=0, tiled=True
        ).astype(jnp.float32),
        lax.psum_scatter(
            d_gate.astype(jnp.bfloat16), "narrow", scatter_dimension=0, tiled=True
        ).astype(jnp.float32),
        lax.psum_scatter(
            d_up.astype(jnp.bfloat16), "narrow", scatter_dimension=0, tiled=True
        ).astype(jnp.float32),
        lax.psum_scatter(
            d_out_t.astype(jnp.bfloat16), "narrow", scatter_dimension=0, tiled=True
        ).astype(jnp.float32),
        lax.psum_scatter(
            d_down_t.astype(jnp.bfloat16), "narrow", scatter_dimension=0, tiled=True
        ).astype(jnp.float32),
    )
    attn_gain_s, q_gain_s, k_gain_s, ffn_gain_s = lax.psum(
        (attn_gain_grad, q_gain_grad, k_gain_grad, ffn_gain_grad), ("narrow", "wide")
    )
    return (
        output,
        d_tokens,
        attn_gain_s,
        d_query_s,
        d_key_s,
        d_value_s,
        q_gain_s,
        k_gain_s,
        d_out_s,
        ffn_gain_s,
        d_gate_s,
        d_up_s,
        d_down_s,
    )


def solution(mesh):
    in_specs = (
        P(("narrow", "wide"), None, None),
        P(),
        P(),
        P(None, "wide"),
        P(None, "wide"),
        P(None, "wide"),
        P(),
        P(),
        P("wide", None),
        P(),
        P(None, "wide"),
        P(None, "wide"),
        P("wide", None),
        P(("narrow", "wide"), None, None),
    )
    out_specs = (
        P(("narrow", "wide"), None, None),
        P(("narrow", "wide"), None, None),
        P(),
        P("narrow", "wide"),
        P("narrow", "wide"),
        P("narrow", "wide"),
        P(),
        P(),
        P("narrow", "wide"),
        P(),
        P("narrow", "wide"),
        P("narrow", "wide"),
        P("narrow", "wide"),
    )
    return jax.shard_map(shards, mesh=mesh, in_specs=in_specs, out_specs=out_specs, check_vma=False)
```

profile of v0, /device:TPU:0, one launch (start us, length us, event | category | flops | bytes accessed | tf_op | source)
XLA Modules:
  0.0 1421.2 jit_solution(2245307094921943791)
XLA Ops:
  10.0 24.9 %all-gather.5.cloned.1.call-done = bf16[256,2,2048]{2,1,0:T(2,128)(2,1)} async-done(((bf16[64,2,2048]{2,1,0:T(2,128)(2,1)}), bf16[256,2,2048]{2,1,0:T(2,128)(2,1)}) %all-gather.5.cloned.1.call-update) | async-done | bytes 2097168 | tf_op jit(solution)/shard_map/all_gather | solution.py:101
  34.9 3.9 multiply_reduce_fusion.6
  40.1 3.9 fusion.120
  48.8 2.6 multiply_reduce_fusion.12
  55.0 3.9 copy.63
  60.1 3.5 multiply_reduce_fusion.9
  65.9 20.7 %all-gather.7.cloned.1.call-done = bf16[2048,2,2,64]{0,3,2,1:T(8,128)(2,1)} async-done(((bf16[256,2,2,64]{0,3,2,1:T(8,128)(2,1)}), bf16[2048,2,2,64]{0,3,2,1:T(8,128)(2,1)}) %all-gather.7.cloned.1.call-update) | async-done | bytes 1048592 | tf_op jit(solution)/shard_map/all_gather | solution.py:121
  88.9 38.2 %all-gather.9.cloned.1.call-done = bf16[2048,2,2,64]{0,3,2,1:T(8,128)(2,1)} async-done(((bf16[256,2,2,64]{0,3,2,1:T(8,128)(2,1)}), bf16[2048,2,2,64]{0,3,2,1:T(8,128)(2,1)}) %all-gather.9.cloned.1.call-update) | async-done | bytes 1048592 | tf_op jit(solution)/shard_map/all_gather | solution.py:120
  128.4 66.2 %while.28 = (s32[]{:T(128)}, bf16[8,256,2,64]{1,3,2,0:T(8,128)(2,1)}, f32[8,2,256]{2,1,0:T(2,128)S(1)}, s32[8]{0:T(128)S(1)}, bf16[2048,2,2,64]{0,3,1,2:T(8,128)...) while((s32[]{:T(128)}, ...), condition=%wide.region_6.7_spmd.clone, body=%wide.region_3.6_spmd.clone.sunk | while | flops 277904896 | bytes 14311615 | solution.py:143
  131.0 2.3 fusion.139
  134.0 2.7 fusion.141
  142.3 2.7 fusion.141
  150.6 2.7 fusion.141
  158.9 2.7 fusion.141
  167.1 2.7 fusion.141
  175.4 2.7 fusion.141
  183.7 2.7 fusion.141
  191.9 2.7 fusion.141
  194.7 2.9 copy.70
  197.6 2.6 reshape.392
  200.1 3.6 convolution_convert_fusion.6
  204.3 4.4 reshape.391
  208.7 4.1 reshape.393
  212.8 41.4 %all-reduce.4.cloned.1.call-done = bf16[512,2048]{1,0:T(8,128)(2,1)} async-done(((bf16[512,2048]{1,0:T(8,128)(2,1)}), bf16[512,2048]{1,0:T(8,128)(2,1)}) %all-reduce.4.cloned.1.call-update) | async-done | bytes 2097168 | tf_op jit(solution)/shard_map/psum | solution.py:146
  254.2 3.5 multiply_reduce_fusion.5
  258.2 11.9 fusion.76
  270.1 6.0 fusion.77
  276.1 12.7 multiply_convert_fusion.1
  288.8 10.7 fusion.78
  299.5 10.1 multiply_reduce_fusion.1
  311.9 51.5 %all-reduce.6.cloned.1.call-done = bf16[512,2048]{1,0:T(8,128)(2,1)} async-done(((bf16[512,2048]{1,0:T(8,128)(2,1)}), bf16[512,2048]{1,0:T(8,128)(2,1)}) %all-reduce.6.cloned.1.call-update) | async-done | bytes 2097168 | tf_op jit(solution)/shard_map/psum | solution.py:173
  363.5 4.3 convolution_convert_fusion.9
  374.4 109.2 %while.29 = (s32[]{:T(128)}, f32[2048,2,2,64]{0,3,2,1:T(8,128)}, f32[2048,2,2,64]{0,3,1,2:T(8,128)}, f32[8,256,2,64]{1,3,0,2:T(8,128)}, s32[8]{0:T(128)S(1)}, /*...) while((s32[]{:T(128)}, f32[2048,2,2,64]{0,3,2,1:T(8,128)}, ...), condition=%wide.region_14.15_spmd.clone, body=%wide.region_12.14_spmd.clone.sunk | while | flops 683441664 | bytes 75909480 | solution.py:215
  378.8 3.1 multiply_reduce_fusion.14
  392.4 3.1 multiply_reduce_fusion.14
  406.1 3.1 multiply_reduce_fusion.14
  419.7 3.1 multiply_reduce_fusion.14
  433.4 3.1 multiply_reduce_fusion.14
  447.1 3.1 multiply_reduce_fusion.14
  460.7 3.1 multiply_reduce_fusion.14
  474.4 3.1 multiply_reduce_fusion.14
  483.6 2.9 convert_element_type.184
  488.1 10.0 convolution_convert_fusion.5
  498.2 3.7 multiply_convert_fusion.4
  501.9 2.7 convert_element_type.192
  504.7 46.0 %reduce-scatter.14.cloned.1.call-done = bf16[256,2,2,64]{0,3,2,1:T(8,128)(2,1)} async-done(((bf16[2048,2,2,64]{0,3,2,1:T(8,128)(2,1)}), bf16[256,2,2,64]{0,3,2,1:T(8,128)(2,1)}) %reduce-scatter.14.cloned.1.call-update) | async-done | bytes 131088 | tf_op jit(solution)/shard_map/reduce_scatter | solution.py:219
  554.5 63.5 %reduce-scatter.16.cloned.1.call-done = bf16[256,2,2,64]{0,3,1,2:T(8,128)(2,1)} async-done(((bf16[2048,2,2,64]{0,3,1,2:T(8,128)(2,1)}), bf16[256,2,2,64]{0,3,1,2:T(8,128)(2,1)}) %reduce-scatter.16.cloned.1.call-update) | async-done | bytes 131088 | tf_op jit(solution)/shard_map/reduce_scatter | solution.py:222
  630.1 3.7 convolution_convert_fusion.4
  634.3 5.3 convolution_convert_fusion.3
  647.6 8.5 convolution_convert_fusion.2
  656.1 8.3 convolution_convert_fusion.1
  666.0 8.4 convolution_convert_fusion
  674.5 4.4 convert_add_fusion
  678.9 40.3 %all-reduce = (f32[2048]{0:T(1024)}, f32[64]{0:T(128)}, f32[64]{0:T(128)}, f32[2048]{0:T(1024)}) all-reduce(f32[2048]{0:T(1024)S(1)} %get-tuple-element.235, f32[64]{0:T(128)S(1)} %copy-done.50, f32[64]{0:T(128)S(1)} %copy-done.49, f32[2048]{0:T(1024)S(1)} %get-tuple-element.233), channel_id=1, replica_groups=mesh['narrow'=8,'wide'=4] {'narrow','wide'}, use_global_device_ids=true, to_apply=%region_22.23 | all-reduce | flops 4224 | bytes 33792 | tf_op jit(solution)/shard_map/psum | solution.py:270
  723.4 58.0 %reduce-scatter.24.cloned.1.call-done = bf16[256,128]{1,0:T(8,128)(2,1)} async-done(((bf16[2048,128]{1,0:T(8,128)(2,1)}), bf16[256,128]{1,0:T(8,128)(2,1)}) %reduce-scatter.24.cloned.1.call-update) | async-done | bytes 65552 | tf_op jit(solution)/shard_map/reduce_scatter | solution.py:254
  782.9 68.9 %reduce-scatter.20.cloned.1.call-done = bf16[256,512]{1,0:T(8,128)(2,1)} async-done(((bf16[2048,512]{1,0:T(8,128)(2,1)}), bf16[256,512]{1,0:T(8,128)(2,1)}) %reduce-scatter.20.cloned.1.call-update) | async-done | bytes 262160 | tf_op jit(solution)/shard_map/reduce_scatter | solution.py:248
  853.7 69.1 %reduce-scatter.26.cloned.1.call-done = bf16[256,512]{1,0:T(8,128)(2,1)} async-done(((bf16[2048,512]{1,0:T(8,128)(2,1)}), bf16[256,512]{1,0:T(8,128)(2,1)}) %reduce-scatter.26.cloned.1.call-update) | async-done | bytes 262160 | tf_op jit(solution)/shard_map/reduce_scatter | solution.py:263
  924.6 31.2 %reduce-scatter.18.cloned.1.call-done = bf16[128,2048]{1,0:T(8,128)(2,1)} async-done(((bf16[512,2048]{1,0:T(8,128)(2,1)}), bf16[128,2048]{1,0:T(8,128)(2,1)}) %reduce-scatter.18.cloned.1.call-update) | async-done | bytes 524304 | tf_op jit(solution)/shard_map/reduce_scatter | solution.py:243
  958.9 149.4 %reduce-scatter.28.cloned.1.call-done = bf16[256,2048]{1,0:T(8,128)(2,1)} async-done(((bf16[2048,2048]{1,0:T(8,128)(2,1)}), bf16[256,2048]{1,0:T(8,128)(2,1)}) %reduce-scatter.28.cloned.1.call-update) | async-done | bytes 1048592 | tf_op jit(solution)/shard_map/reduce_scatter | solution.py:257
  1108.3 2.8 convert_element_type.202
  1111.1 149.2 %reduce-scatter.30.cloned.1.call-done = bf16[256,2048]{1,0:T(8,128)(2,1)} async-done(((bf16[2048,2048]{1,0:T(8,128)(2,1)}), bf16[256,2048]{1,0:T(8,128)(2,1)}) %reduce-scatter.30.cloned.1.call-update) | async-done | bytes 1048592 | tf_op jit(solution)/shard_map/reduce_scatter | solution.py:260
  1260.2 2.8 convert_element_type.204
  1263.0 148.7 %reduce-scatter.32.cloned.1.call-done = bf16[256,2048]{1,0:T(8,128)(2,1)} async-done(((bf16[2048,2048]{1,0:T(8,128)(2,1)}), bf16[256,2048]{1,0:T(8,128)(2,1)}) %reduce-scatter.32.cloned.1.call-update) | async-done | bytes 1048592 | tf_op jit(solution)/shard_map/reduce_scatter | solution.py:266
  1411.7 2.8 convert_element_type.206
  (374 shorter events, 164.0 us)
Async XLA Ops:
  7.2 192.9 %copy-start = (bf16[512,2048]{1,0:T(8,128)(2,1)S(1)}, bf16[512,2048]{1,0:T(8,128)(2,1)}, u32[]{:S(2)}) copy-start(bf16[512,2048]{1,0:T(8,128)(2,1)} %param.26) | copy-start | bytes 6291460
  7.2 32.9 %copy-start.35 = (f32[2048]{0:T(1024)S(1)}, f32[2048]{0:T(1024)}, u32[]{:S(2)}) copy-start(f32[2048]{0:T(1024)} %param.20) | copy-start | bytes 24580
  7.2 27.7 %all-gather.5.cloned.1.call-start = ((), (), s32[]{:S(2)}) async-start(), calls=%async_computation.11 | async-start | bytes 2621440 | tf_op jit(solution)/shard_map/all_gather | solution.py:101
  7.9 78.7 %all-gather.7.cloned.1.call-start = ((), (), s32[]{:S(2)}) async-start(), calls=%async_computation.12 | async-start | bytes 1179648 | tf_op jit(solution)/shard_map/all_gather | solution.py:121
  34.9 10.4 copy-start.31
  38.8 8.2 copy-start.20
  45.4 6.8 copy-start.44
  45.4 7.7 copy-start.48
  45.4 7.8 copy-start.30
  46.9 80.2 %all-gather.9.cloned.1.call-start = ((), (), s32[]{:S(2)}) async-start(), calls=%async_computation.13 | async-start | bytes 1179648 | tf_op jit(solution)/shard_map/all_gather | solution.py:120
  48.8 16.0 %copy-start.26 = (f32[256,32]{0,1:T(8,128)}, f32[256,32]{0,1:T(8,128)S(1)}, u32[]{:S(2)}) copy-start(f32[256,32]{0,1:T(8,128)S(1)} %get-tuple-element.308) | copy-start | bytes 98308
  53.0 155.8 %all-gather.11.cloned.1.call-start = ((), (), s32[]{:S(2)}) async-start(), calls=%async_computation.16 | async-start | bytes 2621440 | tf_op jit(solution)/shard_map/all_gather | solution.py:162
  54.5 199.7 %all-reduce.4.cloned.1.call-start = ((), (), s32[]{:S(2)}) async-start(), calls=%async_computation.14 | async-start | bytes 4194304 | tf_op jit(solution)/shard_map/psum | solution.py:146
  60.1 4.5 copy-start.46
  203.8 159.7 %all-reduce.6.cloned.1.call-start = ((), (), s32[]{:S(2)}) async-start(), calls=%async_computation.17 | async-start | bytes 4194304 | tf_op jit(solution)/shard_map/psum | solution.py:173
  212.8 44.9 %copy-start.41 = (f32[2048]{0:T(1024)S(1)}, f32[2048]{0:T(1024)}, u32[]{:S(2)}) copy-start(f32[2048]{0:T(1024)} %param.27) | copy-start | bytes 24580
  257.7 51.9 %copy-start.3 = (f32[512,2048]{1,0:T(8,128)}, f32[512,2048]{1,0:T(8,128)S(1)}, u32[]{:S(2)}) copy-start(f32[512,2048]{1,0:T(8,128)S(1)} %get-tuple-element.288) | copy-start | bytes 12582916
  257.7 12.4 slice-start
  258.1 11.9 copy-start.18
  258.2 11.9 slice-start.1
  270.1 6.0 copy-start.13
  288.8 10.7 copy-start.51
  311.9 238.8 %reduce-scatter.14.cloned.1.call-start = ((), (), s32[]{:S(2)}) async-start(), calls=%async_computation.18 | async-start | bytes 1179648 | tf_op jit(solution)/shard_map/reduce_scatter | solution.py:219
  383.4 1.6 copy-start.6
  397.1 1.6 copy-start.6
  410.7 1.6 copy-start.6
  424.4 1.6 copy-start.6
  438.1 1.6 copy-start.6
  451.7 1.6 copy-start.6
  465.4 1.6 copy-start.6
  483.6 3.0 copy-start.8
  486.5 131.4 %reduce-scatter.16.cloned.1.call-start = ((), (), s32[]{:S(2)}) async-start(), calls=%async_computation.19 | async-start | bytes 1179648 | tf_op jit(solution)/shard_map/reduce_scatter | solution.py:222
  487.8 231.5 %reduce-scatter.12.cloned.1.call-start = ((), (), s32[]{:S(2)}) async-start(), calls=%async_computation.15 | async-start | bytes 2621440 | tf_op jit(solution)/shard_map/reduce_scatter | solution.py:153
  488.0 10.2 copy-start.9
  488.0 10.2 copy-start.25
  488.0 10.2 copy-start.36
  498.1 53.5 %copy-start.27 = (f32[256,32]{0,1:T(8,128)S(1)}, f32[256,32]{0,1:T(8,128)}, u32[]{:S(2)}) copy-start(f32[256,32]{0,1:T(8,128)} %copy-done.26) | copy-start | bytes 98308
  498.1 53.5 %copy-start.32 = (f32[256,32]{0,1:T(8,128)S(1)}, f32[256,32]{0,1:T(8,128)}, u32[]{:S(2)}) copy-start(f32[256,32]{0,1:T(8,128)} %get-tuple-element.306) | copy-start | bytes 98308
  498.1 53.6 %copy-start.17 = (f32[256,2,2,64]{0,3,2,1:T(8,128)S(1)}, f32[256,2,2,64]{0,3,2,1:T(8,128)}, u32[]{:S(2)}) copy-start(f32[256,2,2,64]{0,3,2,1:T(8,128)} %copy-done.16) | copy-start | bytes 786436
  498.1 53.6 %copy-start.38 = (f32[256,2,2]{0,2,1:T(2,128)S(1)}, f32[256,2,2]{0,2,1:T(2,128)}, u32[]{:S(2)}) copy-start(f32[256,2,2]{0,2,1:T(2,128)} %copy-done.37) | copy-start | bytes 12292
  498.1 53.6 %copy-start.45 = (f32[64]{0:T(128)S(1)}, f32[64]{0:T(128)}, u32[]{:S(2)}) copy-start(f32[64]{0:T(128)} %param.25) | copy-start | bytes 772
  498.1 54.2 %copy-start.43 = (f32[256,2,2]{0,2,1:T(2,128)S(1)}, f32[256,2,2]{0,2,1:T(2,128)}, u32[]{:S(2)}) copy-start(f32[256,2,2]{0,2,1:T(2,128)} %copy-done.42) | copy-start | bytes 12292
  498.1 223.8 %reduce-scatter.22.cloned.1.call-start = ((), (), s32[]{:S(2)}) async-start(), calls=%async_computation.22 | async-start | bytes 589824 | tf_op jit(solution)/shard_map/reduce_scatter | solution.py:251
  554.4 69.4 %copy-start.11 = (f32[256,2,8,64]{0,3,2,1:T(8,128)S(1)}, f32[256,2,8,64]{0,3,2,1:T(8,128)}, u32[]{:S(2)}) copy-start(f32[256,2,8,64]{0,3,2,1:T(8,128)} %copy-done.10) | copy-start | bytes 3145732
  554.4 69.4 %copy-start.34 = (f32[256,2,8]{0,2,1:T(8,128)S(1)}, f32[256,2,8]{0,2,1:T(8,128)}, u32[]{:S(2)}) copy-start(f32[256,2,8]{0,2,1:T(8,128)} %copy-done.33) | copy-start | bytes 49156
  554.4 69.4 %copy-start.47 = (f32[64]{0:T(128)S(1)}, f32[64]{0:T(128)}, u32[]{:S(2)}) copy-start(f32[64]{0:T(128)} %param.24) | copy-start | bytes 772
  554.5 227.0 %reduce-scatter.24.cloned.1.call-start = ((), (), s32[]{:S(2)}) async-start(), calls=%async_computation.23 | async-start | bytes 589824 | tf_op jit(solution)/shard_map/reduce_scatter | solution.py:254
  620.9 3.9 copy-start.40
  622.5 229.4 %reduce-scatter.20.cloned.1.call-start = ((), (), s32[]{:S(2)}) async-start(), calls=%async_computation.21 | async-start | bytes 2359296 | tf_op jit(solution)/shard_map/reduce_scatter | solution.py:248
  630.1 4.2 copy-start.28
  633.8 5.9 copy-start.29
  633.8 6.0 copy-start.12
  633.8 6.0 copy-start.15
  633.8 288.9 %reduce-scatter.26.cloned.1.call-start = ((), (), s32[]{:S(2)}) async-start(), calls=%async_computation.24 | async-start | bytes 2359296 | tf_op jit(solution)/shard_map/reduce_scatter | solution.py:263
  639.6 316.2 %reduce-scatter.18.cloned.1.call-start = ((), (), s32[]{:S(2)}) async-start(), calls=%async_computation.20 | async-start | bytes 2621440 | tf_op jit(solution)/shard_map/reduce_scatter | solution.py:243
  641.1 2.2 copy-start.2
  641.1 2.3 copy-start.22
  645.3 2.3 copy-start.19
  647.5 460.7 %reduce-scatter.28.cloned.1.call-start = ((), (), s32[]{:S(2)}) async-start(), calls=%async_computation.25 | async-start | bytes 9437184 | tf_op jit(solution)/shard_map/reduce_scatter | solution.py:257
  656.1 604.2 %reduce-scatter.30.cloned.1.call-start = ((), (), s32[]{:S(2)}) async-start(), calls=%async_computation.26 | async-start | bytes 9437184 | tf_op jit(solution)/shard_map/reduce_scatter | solution.py:260
  664.5 747.2 %reduce-scatter.32.cloned.1.call-start = ((), (), s32[]{:S(2)}) async-start(), calls=%async_computation.27 | async-start | bytes 9437184 | tf_op jit(solution)/shard_map/reduce_scatter | solution.py:266
  674.5 4.4 copy-start.49
  674.5 4.4 copy-start.50
  957.3 457.3 %copy-start.1 = (bf16[512,2048]{1,0:T(8,128)(2,1)S(1)}, bf16[512,2048]{1,0:T(8,128)(2,1)}, u32[]{:S(2)}) copy-start(bf16[512,2048]{1,0:T(8,128)(2,1)} %param.26) | copy-start | bytes 6291460
  (35 other events, 49.3 us)
Sparse Core Ops, SparseCore 0:
  9.6 25.2 all-gather.4
  47.1 39.5 all-gather.6
  88.7 38.4 all-gather.8
  129.1 21.5 all-gather.10
  203.9 50.2 all-reduce.3
  312.0 51.4 all-reduce.5
  486.7 63.9 reduce-scatter.13
  555.0 62.8 reduce-scatter.15
  620.5 30.4 reduce-scatter.11
  654.5 61.9 reduce-scatter.21
  720.4 60.9 reduce-scatter.23
  785.2 66.5 reduce-scatter.19
  855.8 66.8 reduce-scatter.25
  925.3 30.4 reduce-scatter.17
  959.2 148.9 reduce-scatter.27
  1112.2 147.9 reduce-scatter.29
  1263.7 147.9 reduce-scatter.31
where the time goes:
time: 1430 us; the launch traced here: 1420 us
  waiting for transfers between devices  962 us (67%)
  matrix products  232 us (16%)
  local copies, waits for them, and re-layouts  71.6 us (5%)
  other arithmetic  66.6 us (5%)
  blocking collectives  40.3 us (3%)
  loops' own time  31.8 us (2%)
  between operations  15 us (1%)
    reduce_scatter x1, waiting for transfers between devices, shards(): lax.psum_scatter(d_gate.astype(jnp.bfloat16), 'narrow', scatter_dimension...  149 us
    reduce_scatter x1, waiting for transfers between devices, shards(): lax.psum_scatter(d_up.astype(jnp.bfloat16), 'narrow', scatter_dimension=0...  149 us
    reduce_scatter x1, waiting for transfers between devices, shards(): lax.psum_scatter(d_down_t.astype(jnp.bfloat16), 'narrow', scatter_dimensi...  149 us
    reduce_scatter x1, waiting for transfers between devices, shards(): lax.psum_scatter(d_out_t.astype(jnp.bfloat16), 'narrow', scatter_dimensio...  69.1 us
    reduce_scatter x1, waiting for transfers between devices, shards(): lax.psum_scatter(d_query.astype(jnp.bfloat16), 'narrow', scatter_dimensio...  68.9 us
    reduce_scatter x1, waiting for transfers between devices, shards(): lax.psum_scatter(value_grad_all.astype(jnp.bfloat16), 'narrow', scatter_d...  63.5 us
    reduce_scatter x1, waiting for transfers between devices, shards(): lax.psum_scatter(d_value.astype(jnp.bfloat16), 'narrow', scatter_dimensio...  58 us
    psum x1, waiting for transfers between devices, shards(): lax.psum(mid_part.astype(jnp.bfloat16), 'wide').astype(jnp.float32)  51.5 us
  transfers between devices with their start and end apart: 17, of which 14 were waited for; matrix products, arithmetic and copies ran while one was open for 13% of the time, Pallas kernels for 0%

commit v1 on v0

v1 whole, which is shorter than its diff:
```python
import functools
import math

import jax
import jax.numpy as jnp
from jax import lax
from jax.experimental import pallas as pl
from jax.experimental.pallas import tpu as pltpu
from jax.sharding import PartitionSpec as P

QUERY_HEADS = 32
KEY_VALUE_HEADS = 8
HEAD = 64
HALF = HEAD // 2
GROUP = QUERY_HEADS // KEY_VALUE_HEADS
EPS = 1e-06
SCALE = HEAD ** (-0.5)
AXES = ("narrow", "wide")
TP_BIT = 2
BF = jnp.bfloat16
F32 = jnp.float32
VMEM = 56 * 1024 * 1024

NN = (((1,), (0,)), ((), ()))
NT = (((1,), (1,)), ((), ()))
TN = (((0,), (0,)), ((), ()))


def mm(a, b, dims=NN):
    return lax.dot_general(a, b, dims, preferred_element_type=F32)


def cost(flops, nbytes, trans=0):
    return pl.CostEstimate(flops=int(flops), bytes_accessed=int(nbytes), transcendentals=int(trans))


class Line:
    def __init__(self, at):
        self.at = at
        self.last = []

    def call(self, kernel, *args, grid, in_specs, out_specs, out_shape, scratch=(), cost=None, name=None, deps=()):
        extra = [*self.last, *deps]

        def body(at_ref, *refs):
            kernel(at_ref, *refs[len(extra) :])

        outs = pl.pallas_call(
            body,
            grid_spec=pltpu.PrefetchScalarGridSpec(
                num_scalar_prefetch=1,
                grid=grid,
                in_specs=[pl.BlockSpec(memory_space=pl.ANY)] * len(extra) + list(in_specs),
                out_specs=out_specs,
                scratch_shapes=scratch,
            ),
            out_shape=out_shape,
            compiler_params=pltpu.CompilerParams(vmem_limit_bytes=VMEM),
            cost_estimate=cost,
            name=name,
        )(self.at, *extra, *args)
        self.last = [outs[0] if isinstance(outs, (list, tuple)) else outs]
        return outs


def key_block_mask(j):
    rows = j >> 1
    return (rows & 1) | ((j & 1) << 1) | ((rows >> 1) << 2)


def position_inside(t, share, w):
    u = t // share
    return ((((u & 1) << 1) | (u >> 1)) ^ w) * share + t % share


def positions_in_block(size, share, w, axis):
    shape = (size, 1) if axis == 0 else (1, size)
    return position_inside(lax.broadcasted_iota(jnp.int32, shape, axis), share, w)


def constant(shape):
    return pl.BlockSpec(shape, lambda *_: (0,) * len(shape))


def per_block(shape):
    return pl.BlockSpec(shape, lambda g, i, at: (g, i) + (0,) * (len(shape) - 2))


def per_sequence(shape):
    return pl.BlockSpec(shape, lambda g, *_: (g,) + (0,) * (len(shape) - 1))


def shape_of(shape, dtype=BF):
    return jax.ShapeDtypeStruct(shape, dtype)


def project_kernel(at_ref, a_ref, b_ref, wt_ref, cos_ref, sin_ref, qg_ref, kg_ref, kv_ref, q_ref, raw_ref):
    x = jnp.concatenate([a_ref[0], b_ref[0]], axis=0)
    y = mm(wt_ref[...], x, NT)
    heads = q_ref.shape[2]
    width = heads * HEAD
    raw_ref[0, 0] = y[: width + HEAD]
    c, s = cos_ref[0], sin_ref[0]

    def norm_rope(v, gain):
        r = lax.rsqrt(jnp.mean(v * v, axis=0, keepdims=True) + EPS)
        n = v * r * gain
        a, b = n[:HALF], n[HALF:]
        return a * c - b * s, b * c + a * s

    for h in range(heads):
        a, b = norm_rope(y[h * HEAD : (h + 1) * HEAD], qg_ref[...])
        q_ref[0, 0, h] = (jnp.concatenate([a, b], axis=0) * SCALE).astype(BF)
    a, b = norm_rope(y[width : width + HEAD], kg_ref[...])
    kv = jnp.concatenate([a, b, y[width + HEAD :]], axis=0)
    kv_ref[0] = kv.T.astype(BF)


def project(line, xn, wt, cos, sin, q_gain, k_gain):
    g, b, m = xn[0].shape
    c = wt.shape[0]
    heads = c // HEAD - 2
    table = pl.BlockSpec((1, HALF, b), lambda g, i, at: (i, 0, 0))
    return line.call(
        project_kernel, *xn, wt, cos, sin, q_gain, k_gain,
        grid=(g, 2),
        in_specs=[per_block((1, b // 2, m))] * 2
        + [constant((c, m)), table, table, constant((HEAD, 1)), constant((HEAD, 1))],
        out_specs=[
            per_block((1, b, 2 * HEAD)),
            per_block((1, 1, heads, HEAD, b)),
            per_block((1, 1, (heads + 1) * HEAD, b)),
        ],
        out_shape=[
            shape_of((g, 2 * b, 2 * HEAD)),
            shape_of((g, 2, heads, HEAD, b)),
            shape_of((g, 2, (heads + 1) * HEAD, b), F32),
        ],
        cost=cost(4 * g * b * m * c, 4 * g * b * m + 2 * c * m + 16 * g * b * c),
        name="project",
    )


def attend_kernel(count, share, at_ref, q_ref, *refs):
    kv_refs = refs[:count]
    wo_ref, pb_ref, pa_ref, oa_ref, ob_ref, log_ref, acc_ref, sum_ref = refs[count:]
    n, w = at_ref[0], at_ref[1]
    length = at_ref[3 + pl.program_id(0)]
    heads, _, b = q_ref.shape[2:]
    nq = n ^ (TP_BIT * pl.program_id(1))
    bound = jnp.minimum(nq * b + positions_in_block(b, share, w, 1), length - 1)
    acc_ref[...] = jnp.zeros_like(acc_ref)
    sum_ref[...] = jnp.zeros_like(sum_ref)
    inside = positions_in_block(b, share, w, 0)

    for k, kv_ref in enumerate(kv_refs):
        for tp in range(2):
            nk = n ^ key_block_mask(2 * k + tp)

            @pl.when((nk <= nq) & (nk * b < length))
            def _():
                kv = kv_ref[0, tp * b : (tp + 1) * b, :]
                allowed = nk * b + inside <= bound
                for h in range(heads):
                    scores = mm(kv[:, :HEAD], q_ref[0, 0, h])
                    p = jnp.where(allowed, jnp.exp(scores), 0.0)
                    sum_ref[h : h + 1] += jnp.sum(p, axis=0, keepdims=True)
                    acc_ref[h] += mm(kv, p.astype(BF), TN)

    outs = []
    for h in range(heads):
        total = sum_ref[h : h + 1]
        outs.append(acc_ref[h, HEAD:, :] / total)
    log_ref[0, 0] = jnp.log(sum_ref[...])
    o = jnp.concatenate(outs, axis=0).T.astype(BF)
    oa_ref[0] = o[: b // 2]
    ob_ref[0] = o[b // 2 :]
    part = mm(o, wo_ref[...]).astype(BF)
    pa_ref[0] = part[: b // 2]
    pb_ref[0] = part[b // 2 :]


def attend(line, q, kvs, w_out, share):
    g, _, heads, _, b = q.shape
    keys = 2 * b * len(kvs)
    m = w_out.shape[1]
    width = heads * HEAD
    return line.call(
        functools.partial(attend_kernel, len(kvs), share), q, *kvs, w_out,
        grid=(g, 2),
        in_specs=[per_block((1, 1, heads, HEAD, b))]
        + [per_sequence((1, 2 * b, 2 * HEAD))] * len(kvs)
        + [pl.BlockSpec((width, m), lambda g, i, at: (at[2], 0))],
        out_specs=[per_block((1, b // 2, m))] * 2
        + [per_block((1, b // 2, width))] * 2
        + [per_block((1, 1, heads, b))],
        out_shape=[shape_of((g, b, m))] * 2
        + [shape_of((g, b, width))] * 2
        + [shape_of((g, 2, heads, b), F32)],
        scratch=[pltpu.VMEM((heads, 2 * HEAD, b), F32), pltpu.VMEM((heads, b), F32)],
        cost=cost(
            2 * g * 2 * b * keys * heads * 192 + 4 * g * b * width * m,
            2 * g * (keys * 2 * HEAD + 2 * b * m) + 2 * width * m,
            g * b * keys * heads,
        ),
        name="attend",
    )


def attend_back_kernel(count, share, at_ref, dha_ref, dhb_ref, q_ref, *refs):
    kv_refs, refs = refs[:count], refs[count:]
    wo_ref, oa_ref, ob_ref, log_ref, raw_ref, cos_ref, sin_ref, qg_ref, dqa_ref, dqb_ref = refs[:10]
    dkv_refs, dqg_ref = refs[10 : 10 + count], refs[10 + count]
    q_ext, do_ext, delta, dq_acc, dkv_acc = refs[11 + count :]
    n, w = at_ref[0], at_ref[1]
    at_g, i = pl.program_id(0), pl.program_id(1)
    length = at_ref[3 + at_g]
    heads, _, b = q_ref.shape[2:]
    nq = n ^ (TP_BIT * i)
    bound = jnp.minimum(nq * b + positions_in_block(b, share, w, 1), length - 1)
    inside = positions_in_block(b, share, w, 0)

    @pl.when(i == 0)
    def _():
        dkv_acc[...] = jnp.zeros_like(dkv_acc)

    @pl.when((i == 0) & (at_g == 0))
    def _():
        dqg_ref[...] = jnp.zeros_like(dqg_ref)

    dh = jnp.concatenate([dha_ref[0], dhb_ref[0]], axis=0)
    do = mm(wo_ref[...], dh, NT).astype(BF)
    o = jnp.concatenate([oa_ref[0], ob_ref[0]], axis=0).astype(F32).T
    none = jnp.zeros((HEAD, b), BF)
    for h in range(heads):
        do_h = do[h * HEAD : (h + 1) * HEAD]
        o_h = o[h * HEAD : (h + 1) * HEAD]
        delta[h : h + 1] = jnp.sum(do_h.astype(F32) * o_h, axis=0, keepdims=True)
        do_ext[h] = jnp.concatenate([none, do_h], axis=0)
        q_ext[h] = jnp.concatenate([q_ref[0, 0, h], none], axis=0)
    dq_acc[...] = jnp.zeros_like(dq_acc)

    for k, kv_ref in enumerate(kv_refs):
        for tp in range(2):
            nk = n ^ key_block_mask(2 * k + tp)

            @pl.when((nk <= nq) & (nk * b < length) & (nq * b < length))
            def _():
                kv = kv_ref[0, tp * b : (tp + 1) * b, :]
                allowed = nk * b + inside <= bound
                total = jnp.zeros((b, 2 * HEAD), F32)
                for h in range(heads):
                    scores = mm(kv, q_ext[h])
                    p = jnp.where(allowed, jnp.exp(scores - log_ref[0, 0, h : h + 1]), 0.0)
                    dp = mm(kv, do_ext[h])
                    ds = (p * (dp - delta[h : h + 1])).astype(BF)
                    dq_acc[h] += mm(kv, ds, TN)
                    total += mm(ds, q_ext[h], NT) + mm(p.astype(BF), do_ext[h], NT)
                rows = (2 * k + tp) * b
                dkv_acc[rows : rows + b, :] += total

    c, s = cos_ref[0], sin_ref[0]
    parts = []
    gain_sum = jnp.zeros((HEAD, b), F32)
    for h in range(heads):
        dq = dq_acc[h, :HEAD, :] * SCALE
        e1, e2 = dq[:HALF], dq[HALF:]
        e = jnp.concatenate([e1 * c + e2 * s, e2 * c - e1 * s], axis=0)
        v = raw_ref[0, 0, h * HEAD : (h + 1) * HEAD, :]
        r = lax.rsqrt(jnp.mean(v * v, axis=0, keepdims=True) + EPS)
        unit = v * r
        ge = qg_ref[...] * e
        parts.append(r * (ge - unit * jnp.mean(ge * unit, axis=0, keepdims=True)))
        gain_sum += e * unit
    dq = jnp.concatenate(parts, axis=0).T.astype(BF)
    dqa_ref[0] = dq[: b // 2]
    dqb_ref[0] = dq[b // 2 :]
    dqg_ref[...] += gain_sum

    @pl.when(i == 1)
    def _():
        for k, ref in enumerate(dkv_refs):
            ref[0] = dkv_acc[2 * k * b : 2 * (k + 1) * b, :].astype(BF)


def attend_back(line, dh, q, kvs, w_out, o, log, raw, cos, sin, q_gain, share):
    g, _, heads, _, b = q.shape
    keys = 2 * b * len(kvs)
    m = w_out.shape[1]
    width = heads * HEAD
    half_rows = per_block((1, b // 2, width))
    table = pl.BlockSpec((1, HALF, b), lambda g, i, at: (i, 0, 0))
    return line.call(
        functools.partial(attend_back_kernel, len(kvs), share),
        *dh, q, *kvs, w_out, *o, log, raw, cos, sin, q_gain,
        grid=(g, 2),
        in_specs=[per_block((1, b // 2, m))] * 2
        + [per_block((1, 1, heads, HEAD, b))]
        + [per_sequence((1, 2 * b, 2 * HEAD))] * len(kvs)
        + [
            pl.BlockSpec((width, m), lambda g, i, at: (at[2], 0)),
            half_rows,
            half_rows,
            per_block((1, 1, heads, b)),
            per_block((1, 1, width, b)),
            table,
            table,
            constant((HEAD, 1)),
        ],
        out_specs=[half_rows, half_rows]
        + [per_sequence((1, 2 * b, 2 * HEAD))] * len(kvs)
        + [constant((HEAD, b))],
        scratch=[
            pltpu.VMEM((heads, 2 * HEAD, b), BF),
            pltpu.VMEM((heads, 2 * HEAD, b), BF),
            pltpu.VMEM((heads, b), F32),
            pltpu.VMEM((heads, 2 * HEAD, b), F32),
            pltpu.VMEM((keys, 2 * HEAD), F32),
        ],
        out_shape=[shape_of((g, b, width))] * 2
        + [shape_of((g, 2 * b, 2 * HEAD))] * len(kvs)
        + [shape_of((HEAD, b), F32)],
        cost=cost(
            2 * g * 2 * b * keys * heads * 640 + 4 * g * b * width * m,
            2 * g * (keys * 4 * HEAD + 2 * b * m) + 2 * width * m,
            g * b * keys * heads,
        ),
        name="attend_back",
    )


def project_back_kernel(count, at_ref, *refs):
    dkv_refs = refs[:count]
    (
        dqa_ref, dqb_ref, raw_ref, xa_ref, xb_ref, wt_ref, cos_ref, sin_ref, kg_ref,
        dxb_ref, dxa_ref, dkva_ref, dkvb_ref, dkg_ref, dag_ref,
    ) = refs[count:]

    @pl.when((pl.program_id(0) == 0) & (pl.program_id(1) == 0))
    def _():
        dkg_ref[...] = jnp.zeros_like(dkg_ref)
        dag_ref[...] = jnp.zeros_like(dag_ref)

    total = dkv_refs[0][0].astype(F32)
    for ref in dkv_refs[1:]:
        total += ref[0].astype(F32)
    t = total.T
    half = total.shape[0] // 2
    c, s = cos_ref[0], sin_ref[0]
    e1, e2 = t[:HALF], t[HALF:HEAD]
    e = jnp.concatenate([e1 * c + e2 * s, e2 * c - e1 * s], axis=0)
    v = raw_ref[0, 0]
    r = lax.rsqrt(jnp.mean(v * v, axis=0, keepdims=True) + EPS)
    unit = v * r
    ge = kg_ref[...] * e
    dk = r * (ge - unit * jnp.mean(ge * unit, axis=0, keepdims=True))
    dkg_ref[...] += e * unit
    dkv = jnp.concatenate([dk, t[HEAD:]], axis=0).T.astype(BF)
    dkva_ref[0] = dkv[:half]
    dkvb_ref[0] = dkv[half:]
    width = dqa_ref.shape[2]
    gain_sum = jnp.zeros(dag_ref.shape, F32)
    for rows, dq_ref, x_ref, dx_ref in (
        (slice(0, half), dqa_ref, xa_ref, dxa_ref),
        (slice(half, 2 * half), dqb_ref, xb_ref, dxb_ref),
    ):
        dx = mm(dq_ref[0], wt_ref[:width]) + mm(dkv[rows], wt_ref[width:])
        dx_ref[0] = dx.astype(BF)
        gain_sum += jnp.sum(dx * x_ref[0].astype(F32), axis=0, keepdims=True)
    dag_ref[...] += gain_sum


def project_back(line, dkvs, dq, raw, xn, wt, cos, sin, k_gain):
    g, b, m = xn[0].shape
    c = wt.shape[0]
    width = dq[0].shape[2]
    heads = width // HEAD
    table = pl.BlockSpec((1, HALF, b), lambda g, i, at: (i, 0, 0))
    return line.call(
        functools.partial(project_back_kernel, len(dkvs)),
        *dkvs, *dq, raw, *xn, wt, cos, sin, k_gain,
        grid=(g, 2),
        in_specs=[per_block((1, b, 2 * HEAD))] * len(dkvs)
        + [per_block((1, b // 2, width))] * 2
        + [pl.BlockSpec((1, 1, HEAD, b), lambda g, i, at: (g, i, heads, 0))]
        + [per_block((1, b // 2, m))] * 2
        + [constant((c, m)), table, table, constant((HEAD, 1))],
        out_specs=[per_block((1, b // 2, m))] * 2
        + [per_block((1, b // 2, 2 * HEAD))] * 2
        + [constant((HEAD, b)), constant((1, m))],
        out_shape=[shape_of((g, b, m))] * 2
        + [shape_of((g, b, 2 * HEAD))] * 2
        + [shape_of((HEAD, b), F32), shape_of((1, m), F32)],
        cost=cost(4 * g * b * m * c, 8 * g * b * m + 2 * c * m + 16 * g * b * c),
        name="project_back",
    )


def ffn_kernel(
    tiles, at_ref, ha_ref, hb_ref, ga_ref, gb_ref, wg_ref, wu_ref, wd_ref, wgr_ref, wur_ref,
    db_ref, da_ref, act_ref, dgate_ref, dup_ref, keep_ref,
):
    t = pl.program_id(0)
    rows = ha_ref.shape[0]

    @pl.when(t < tiles)
    def _():
        for k, (h_ref, g_ref) in enumerate(((ha_ref, ga_ref), (hb_ref, gb_ref))):
            at = slice(k * rows, (k + 1) * rows)
            gate = mm(h_ref[...], wg_ref[...])
            up = mm(h_ref[...], wu_ref[...])
            dact = mm(g_ref[...], wd_ref[...], NT)
            sig = 1.0 / (1.0 + jnp.exp(-gate))
            silu = gate * sig
            act_ref[at, :] = (silu * up).astype(BF)
            dgate = (dact * up * (sig * (1.0 + gate * (1.0 - sig)))).astype(BF)
            dup = (dact * silu).astype(BF)
            dgate_ref[at, :] = dgate
            dup_ref[at, :] = dup
            keep_ref[t, 0, at, :] = dgate
            keep_ref[t, 1, at, :] = dup

    @pl.when(t >= tiles)
    def _():
        tile = keep_ref.shape[3]
        for k, d_ref in enumerate((da_ref, db_ref)):
            at = slice(k * rows, (k + 1) * rows)
            total = None
            for u in range(tiles):
                columns = slice(u * tile, (u + 1) * tile)
                part = mm(keep_ref[u, 0, at, :], wgr_ref[:, columns], NT)
                part += mm(keep_ref[u, 1, at, :], wur_ref[:, columns], NT)
                total = part if total is None else total + part
            d_ref[...] = total.astype(BF)


def ffn(line, hn, g, w_gate, w_up, w_down):
    r, m = hn[0].shape
    hidden = w_gate.shape[1] // 2
    tile, block = 256, 256
    tiles = hidden // tile

    def forward(t):
        return jnp.minimum(t, tiles - 1)

    def backward(t):
        return jnp.maximum(t - tiles, 0)

    columns = pl.BlockSpec((m, tile), lambda t, at: (0, at[2] * tiles + forward(t)))
    block_rows = pl.BlockSpec((block, hidden), lambda t, at: (backward(t), at[2]))
    d_block = pl.BlockSpec((r, block), lambda t, at: (0, backward(t)))
    hidden_block = pl.BlockSpec((2 * r, tile), lambda t, at: (0, forward(t)))
    return line.call(
        functools.partial(ffn_kernel, tiles), *hn, *g, w_gate, w_up, w_down, w_gate, w_up,
        grid=(tiles + m // block,),
        in_specs=[constant((r, m))] * 4
        + [
            columns,
            columns,
            pl.BlockSpec((tile, m), lambda t, at: (at[2] * tiles + forward(t), 0)),
            block_rows,
            block_rows,
        ],
        out_specs=[d_block, d_block, hidden_block, hidden_block, hidden_block],
        scratch=[pltpu.VMEM((tiles, 2, 2 * r, tile), BF)],
        out_shape=[shape_of((r, m))] * 2 + [shape_of((2 * r, hidden))] * 3,
        cost=cost(20 * r * m * hidden, 10 * m * hidden + 12 * r * m + 12 * r * hidden),
        name="ffn",
    )


def down_kernel(at_ref, act_ref, wd_ref, b_ref, a_ref):
    r = a_ref.shape[0]
    y = mm(act_ref[...], wd_ref[...]).astype(BF)
    a_ref[...] = y[:r]
    b_ref[...] = y[r:]


def down(line, act, w_down):
    rows, hidden = act.shape
    m = w_down.shape[1]
    block = 256
    out = pl.BlockSpec((rows // 2, block), lambda t, at: (0, t))
    return line.call(
        down_kernel, act, w_down,
        grid=(m // block,),
        in_specs=[
            constant((rows, hidden)),
            pl.BlockSpec((hidden, block), lambda t, at: (at[2], t)),
        ],
        out_specs=[out, out],
        out_shape=[shape_of((rows // 2, m))] * 2,
        cost=cost(2 * rows * hidden * m, 2 * (rows * hidden + hidden * m + rows * m)),
        name="down",
    )


def chip_sum_kernel(at_ref, a_ref, b_ref, *out_refs):
    share = out_refs[0].shape[1]
    for k, ref in enumerate(out_refs):
        at = slice(k * share, (k + 1) * share)
        ref[0] = (a_ref[0, at, :].astype(F32) + b_ref[0, at, :].astype(F32)).astype(BF)


def chip_sum(line, a, b):
    g, rows, m = a.shape
    return line.call(
        chip_sum_kernel, a, b,
        grid=(g,),
        in_specs=[per_sequence((1, rows, m))] * 2,
        out_specs=[per_sequence((1, rows // 4, m))] * 4,
        out_shape=[shape_of((g, rows // 4, m))] * 4,
        cost=cost(g * rows * m, 6 * g * rows * m),
        name="chip_sum",
    )


def stack_kernel(at_ref, *refs):
    share = refs[0].shape[1]
    for k, ref in enumerate(refs[:-1]):
        refs[-1][0, k * share : (k + 1) * share, :] = ref[0]


def stack(line, pieces):
    g, share, m = pieces[0].shape
    count = len(pieces)
    return line.call(
        stack_kernel, *pieces,
        grid=(g,),
        in_specs=[per_sequence((1, share, m))] * count,
        out_specs=per_sequence((1, count * share, m)),
        out_shape=shape_of((g, count * share, m)),
        cost=cost(0, 4 * g * count * share * m),
        name="stack",
    )


def mask_kernel(n_rows, share, at_ref, g_ref, out_ref):
    length = at_ref[3 + pl.program_id(0)]
    first = at_ref[0] * n_rows + at_ref[1] * share
    p = first + lax.broadcasted_iota(jnp.int32, (share, 1), 0)
    out_ref[0] = jnp.where(p < length, g_ref[0].astype(F32), 0.0).astype(BF)


def mask(line, grad, b):
    g, share, m = grad.shape
    return line.call(
        functools.partial(mask_kernel, b, share), grad,
        grid=(g,),
        in_specs=[per_sequence((1, share, m))],
        out_specs=per_sequence((1, share, m)),
        out_shape=shape_of((g, share, m)),
        cost=cost(g * share * m, 4 * g * share * m),
        name="mask",
    )


def middle_kernel(at_ref, own_ref, x_ref, z_ref, d_ref, tok_ref, gain_ref, hn_ref, h_ref):
    h = tok_ref[0].astype(F32)
    for ref in (own_ref, x_ref, z_ref, d_ref):
        h += ref[0].astype(F32)
    h_ref[0] = h
    r = lax.rsqrt(jnp.mean(h * h, axis=-1, keepdims=True) + EPS)
    hn_ref[0] = (h * r * gain_ref[...]).astype(BF)


def middle(line, pieces, tok, gain):
    g, share, m = tok.shape
    piece = per_sequence((1, share, m))
    return line.call(
        middle_kernel, *pieces, tok, gain,
        grid=(g,),
        in_specs=[piece] * 5 + [constant((1, m))],
        out_specs=[piece] * 2,
        out_shape=[shape_of((g, share, m)), shape_of((g, share, m), F32)],
        cost=cost(10 * g * share * m, 16 * g * share * m),
        name="middle",
    )


def middle_back_kernel(at_ref, own_ref, x_ref, z_ref, d_ref, h_ref, g_ref, gain_ref, low_ref, dh_ref, dg_ref):
    e = own_ref[0].astype(F32)
    for ref in (x_ref, z_ref, d_ref):
        e += ref[0].astype(F32)
    h = h_ref[0]
    r = lax.rsqrt(jnp.mean(h * h, axis=-1, keepdims=True) + EPS)
    unit = h * r
    ge = gain_ref[...] * e
    dh = g_ref[0].astype(F32) + r * (ge - unit * jnp.mean(ge * unit, axis=-1, keepdims=True))
    dh_ref[0] = dh
    low_ref[0] = dh.astype(BF)

    @pl.when(pl.program_id(0) == 0)
    def _():
        dg_ref[...] = jnp.zeros_like(dg_ref)

    dg_ref[...] += jnp.sum(e * unit, axis=0, keepdims=True)


def middle_back(line, pieces, h, grad, gain):
    g, share, m = h.shape
    piece = per_sequence((1, share, m))
    return line.call(
        middle_back_kernel, *pieces, h, grad, gain,
        grid=(g,),
        in_specs=[piece] * 6 + [constant((1, m))],
        out_specs=[piece, piece, constant((1, m))],
        out_shape=[shape_of((g, share, m)), shape_of((g, share, m), F32), shape_of((1, m), F32)],
        cost=cost(20 * g * share * m, 20 * g * share * m),
        name="middle_back",
    )


def grad_kernel(received, final, at_ref, la_ref, lb_ref, ra_ref, rb_ref, *refs):
    out_ref = refs[-1]

    def own():
        total = mm(la_ref[...], ra_ref[...], TN) + mm(lb_ref[...], rb_ref[...], TN)
        for ref in refs[:received]:
            total += ref[...].astype(F32)
        return total

    if final:

        @pl.when(pl.program_id(0) == 0)
        def _():
            out_ref[...] = own()

        @pl.when(pl.program_id(0) == 1)
        def _():
            out_ref[...] = refs[received][...].astype(F32)
    else:
        out_ref[...] = own().astype(BF)


def grad_stage(line, masks, left, right, received, peer=None):
    r, m = left[0].shape
    c = right[0][0].shape[1]
    count = lax.axis_size("narrow")
    block = m // count
    first, final = masks[0], peer is not None
    step = masks[1] - masks[0] if len(masks) > 1 else 0
    assert list(masks) == [first + k * step for k in range(len(masks))]

    def which(k):
        return 0 if final else k

    if block % 128:
        left = [jnp.moveaxis(x.reshape(r, count, block), 1, 0) for x in left]
        left_spec = pl.BlockSpec(
            (None, r, block), lambda k, at: (at[0] ^ (first + which(k) * step), 0, 0)
        )
    else:
        left_spec = pl.BlockSpec((r, block), lambda k, at: (0, at[0] ^ (first + which(k) * step)))
    arrays = [left[0], left[1], right[0][0], right[1][0]]
    specs = [left_spec, left_spec] + [
        pl.BlockSpec((r, c), lambda k, at, rows=rows: (rows, 0)) for _, rows in right
    ]
    for x, begin in received + ([(peer, 0)] if final else []):
        arrays.append(x)
        specs.append(
            pl.BlockSpec((None, block, c), lambda k, at, begin=begin: (begin + which(k), 0, 0))
        )
    if final:
        grid = (2,)
        out_spec = pl.BlockSpec((block, c), lambda k, at: (0, k ^ at[2]))
        out_shape = shape_of((block, 2 * c), F32)
    else:
        grid = (len(masks),)
        out_spec = pl.BlockSpec((None, block, c), lambda k, at: (k, 0, 0))
        out_shape = shape_of((len(masks), block, c))
    return line.call(
        functools.partial(grad_kernel, len(received), final), *arrays,
        grid=grid,
        in_specs=specs,
        out_specs=out_spec,
        out_shape=out_shape,
        cost=cost(
            4 * r * block * c * len(masks),
            4 * r * (block * len(masks) + c) + (2 + 2 * len(received)) * len(masks) * block * c,
        ),
        name="grad",
    )


def swap(x, narrow_mask, wide_mask):
    wide = lax.axis_size("wide")
    count = lax.axis_size("narrow") * wide
    mask = narrow_mask * wide + wide_mask
    return lax.ppermute(x, AXES, [(d, d ^ mask) for d in range(count)])


PEERS = ((0, 2), (TP_BIT, 0), (TP_BIT, 2))


def send(x):
    return [x] + [swap(x, *peer) for peer in PEERS]


def gathered(line, pieces):
    a = stack(line, pieces)
    return a, swap(a, 0, 1)


def scatter(line, a, b):
    pieces = chip_sum(line, a, b)
    return [pieces[0]] + [swap(piece, *peer) for piece, peer in zip(pieces[1:], PEERS)]


def added(pieces):
    return functools.reduce(lambda x, y: x + y, [p.astype(F32) for p in pieces])


def row_masks(count):
    return [(k & 1) | ((k >> 1) << 2) for k in range(count // 2)]


def add_kernel(at_ref, x_ref, y_ref, out_ref):
    out_ref[...] = x_ref[...] + y_ref[...]


class Total:
    def __init__(self, line, x):
        self.line, self.x = line, x
        narrow = [1 << k for k in range(lax.axis_size("narrow").bit_length() - 1)]
        wide = [1 << k for k in range(lax.axis_size("wide").bit_length() - 1)]
        self.steps = [(0, k) for k in wide] + [(TP_BIT, 0)] + [(k, 0) for k in narrow if k != TP_BIT]
        self.sent = swap(x, *self.steps.pop(0))

    def step(self):
        whole = constant(self.x.shape)
        self.x = self.line.call(
            add_kernel, self.x, self.sent,
            grid=(1,), in_specs=[whole, whole], out_specs=whole, out_shape=shape_of(self.x.shape, F32), name="add",
        )
        self.sent = swap(self.x, *self.steps.pop(0)) if self.steps else None

    def rest(self):
        while self.sent is not None:
            self.step()
        return self.x


class WeightGrad:
    def __init__(self, line, count, left, right):
        self.line, self.left, self.right = line, left, right
        self.masks = list(range(count))
        self.bits = [1] + [
            bit for k in range(1, count.bit_length()) if 1 < (bit := count >> k) < count and bit != TP_BIT
        ]
        self.received = []

    def step(self):
        bit = self.bits.pop(0)
        away = [k for k in self.masks if k & bit]
        begin = self.masks.index(away[0])
        self.masks = [k for k in self.masks if not k & bit]
        part = grad_stage(self.line, away, self.left, self.right, [(x, begin) for x in self.received])
        self.received.append(swap(part, bit, 0))

    def rest(self):
        while self.bits:
            self.step()

    def last(self):
        self.rest()
        part = grad_stage(self.line, [TP_BIT], self.left, self.right, [(x, 1) for x in self.received])
        self.peer = swap(part, TP_BIT, 0)

    def finish(self):
        received = [(x, 0) for x in self.received]
        return grad_stage(self.line, [0], self.left, self.right, received, self.peer)


def unit_rows(v):
    r = lax.rsqrt(jnp.mean(v * v, axis=-1, keepdims=True) + EPS)
    return v * r, r


def norm_back(unit, r, gain, grad):
    ge = gain * grad
    return r * (ge - unit * jnp.mean(ge * unit, axis=-1, keepdims=True))


def shards(
    tokens, lengths, attn_gain, w_query, key_matrix, value_matrix, q_gain, k_gain, w_out, ffn_gain,
    w_gate, w_up, w_down, out_grad,
):
    n, w = lax.axis_index("narrow"), lax.axis_index("wide")
    count = lax.axis_size("narrow")
    share, seqs, m = tokens.shape
    b = share * lax.axis_size("wide")
    half = (n // TP_BIT) % 2
    width = w_query.shape[1] // 2
    kv_width = key_matrix.shape[1] // 2

    def own_columns(x, size):
        return lax.dynamic_slice_in_dim(x, half * size, size, 1)

    wt = jnp.concatenate(
        [own_columns(w_query, width), own_columns(key_matrix, kv_width), own_columns(value_matrix, kv_width)],
        axis=1,
    ).T
    inside = position_inside(jnp.arange(b, dtype=jnp.int32), share, w)
    positions = jnp.stack([n * b + inside, (n ^ TP_BIT) * b + inside]).astype(F32)
    freqs = jnp.exp(-math.log(10000.0) * jnp.arange(HALF, dtype=F32) * 2.0 / HEAD)
    angles = positions[:, None, :] * freqs[None, :, None]
    cos, sin = jnp.cos(angles), jnp.sin(angles)
    qg, kg = q_gain[:, None], k_gain[:, None]
    line = Line(jnp.concatenate([jnp.stack([n, w, half]).astype(jnp.int32), lengths]))
    masks = row_masks(count)
    rows = seqs * b
    shape = (seqs, b, m)

    def flat(pair):
        return tuple(x.reshape(rows, x.shape[-1]) for x in pair)

    def whole(pair):
        return tuple((x, 0) for x in flat(pair))

    def halves(x):
        return ((x, 0), (x, 1))

    def weight(left, right):
        return WeightGrad(line, count, flat(left), right)

    tok = jnp.moveaxis(tokens, 1, 0)
    out_grad = jnp.moveaxis(out_grad, 1, 0)

    tok_unit, tok_r = unit_rows(tok.astype(F32))
    xn = gathered(line, send((tok_unit * attn_gain).astype(BF)))
    kv, q, raw = project(line, xn, wt, cos, sin, qg, kg)
    kvs = [swap(kv, k, 0) if k else kv for k in masks]
    grad = mask(line, out_grad, b)
    grad_pieces = send(grad)
    pb, pa, oa, ob, log = attend(line, q, kvs, w_out, share)
    pb = swap(pb, 0, 1)
    pieces = scatter(line, pa, pb)
    g_all = gathered(line, grad_pieces)
    hn, h = middle(line, pieces, tok, ffn_gain[None])
    hn = gathered(line, send(hn))

    db, da, act, dgate, dup = ffn(line, flat(hn), flat(g_all), w_gate, w_up, w_down)
    db = swap(db, 0, 1)
    d_down = weight(g_all, halves(act))
    d_gate, d_up = weight(hn, halves(dgate)), weight(hn, halves(dup))
    d_down.step()
    pieces = scatter(line, da.reshape(shape), db.reshape(shape))
    d_gate.step()
    dhl, dh, ffn_gain_grad = middle_back(line, pieces, h, grad, ffn_gain[None])
    pieces = send(dhl)
    yb, ya = down(line, act, w_down)
    yb = swap(yb, 0, 1)
    dhl = gathered(line, pieces)
    d_down.rest()

    back = attend_back(line, dhl, q, kvs, w_out, (oa, ob), log, raw, cos, sin, qg, share)
    dq, dkvs, dqg = back[:2], back[2:-1], back[-1]
    dkvs = [swap(x, k, 0) if k else x for x, k in zip(dkvs, masks)]
    d_gate.rest()
    d_up.step()
    dxb, dxa, dkva, dkvb, dkg, dag = project_back(line, dkvs, dq, raw, xn, wt, cos, sin, kg)
    dxb = swap(dxb, 0, 1)
    d_query = weight(xn, whole(dq))
    d_query.step()
    pieces = scatter(line, dxa, dxb)
    gains = jnp.concatenate(
        [dag[0] / attn_gain, ffn_gain_grad[0], jnp.sum(dqg, axis=1), jnp.sum(dkg, axis=1)]
    )
    gains = Total(line, gains.reshape(-1, 128))
    d_kv = weight(xn, whole((dkva, dkvb)))
    d_kv.step()
    gains.step()
    d_out = weight(dhl, whole((oa, ob)))
    d_out.step()
    gains.step()
    y_pieces = scatter(line, ya.reshape(shape), yb.reshape(shape))
    d_up.rest()
    gains.step()
    d_query.rest()
    d_down.last()
    d_kv.rest()
    d_out.rest()
    d_gate.last()
    dxn = added(pieces)
    d_tokens = dh + norm_back(tok_unit, tok_r, attn_gain, dxn)
    mixed = (h + added(y_pieces)).astype(BF)
    down_grad = d_down.finish()
    gate_grad = d_gate.finish()
    d_up.last()
    d_query.last()
    d_kv.last()
    d_out.last()
    gains.step()
    up_grad = d_up.finish()
    query_grad = d_query.finish()
    kv_grad = d_kv.finish()
    out_grad_t = d_out.finish()
    gains = gains.rest().reshape(-1)
    kv_grad = kv_grad.reshape(-1, 2, 2, kv_width)
    return (
        jnp.moveaxis(mixed, 0, 1),
        jnp.moveaxis(d_tokens, 0, 1),
        gains[:m],
        query_grad,
        kv_grad[:, :, 0].reshape(-1, 2 * kv_width),
        kv_grad[:, :, 1].reshape(-1, 2 * kv_width),
        gains[2 * m : 2 * m + HEAD],
        gains[2 * m + HEAD :],
        out_grad_t,
        gains[m : 2 * m],
        gate_grad,
        up_grad,
        down_grad,
    )


def solution(mesh):
    rows = P(AXES, None, None)
    columns = P(None, "wide")
    block = P("narrow", "wide")
    in_specs = (
        rows, P(), P(), columns, columns, columns, P(), P(), P("wide", None), P(), columns, columns,
        P("wide", None), rows,
    )
    out_specs = (
        rows, rows, P(), block, block, block, P(), P(), block, P(), block, block, block,
    )
    return jax.shard_map(shards, mesh=mesh, in_specs=in_specs, out_specs=out_specs, check_vma=False)
```

time: 1430 us -> 644 us (0.45)
  waiting for transfers between devices: 962 us -> 250 us
  Pallas kernels: 0 us -> 242 us
  matrix products: 232 us -> 0 us
  starting transfers between devices: 2.31 us -> 95 us
  other arithmetic: 66.6 us -> 9.15 us
  blocking collectives: 40.3 us -> 0 us
  local copies, waits for them, and re-layouts: 71.6 us -> 36.8 us
  loops' own time: 31.8 us -> 0 us
    reduce_scatter x11 -> x0, waiting for transfers between devices: 784 us -> none  [the longest x1 149 us: shards(): lax.psum_scatter(d_gate.astype(jnp.bfloat16), 'narrow', scatter_dimension...]
    ppermute x0 -> x61, waiting for transfers between devices: none -> 250 us  [swap(): return lax.ppermute(x, AXES, [(d, d ^ mask) for d in range(count)])]
    pallas_call x0 -> x46, Pallas kernels: none -> 242 us  [call(): pl.pallas_call(body, grid_spec=pltpu.PrefetchScalarGridSpec(num_scalar_pr...]
    dot_general x77 -> x0, matrix products: 232 us -> none  [the longest x16 43 us: head_scores(): jnp.einsum('qsd,ksd->sqk', query_h, key_h, preferred_element_type=jnp.flo...]
    ppermute x0 -> x61, starting transfers between devices: none -> 95 us  [swap(): return lax.ppermute(x, AXES, [(d, d ^ mask) for d in range(count)])]
    psum x2 -> x0, waiting for transfers between devices: 92.9 us -> none  [the longest x1 51.5 us: shards(): lax.psum(mid_part.astype(jnp.bfloat16), 'wide').astype(jnp.float32)]
    all_gather x4 -> x0, waiting for transfers between devices: 83.8 us -> none  [the longest x1 38.2 us: shards(): lax.all_gather(key_rows, 'narrow', axis=0, tiled=True)]
    psum x1 -> x0, blocking collectives: 40.3 us -> none  [shards(): lax.psum((attn_gain_grad, q_gain_grad, k_gain_grad, ffn_gain_grad), ('nar...]
  transfers between devices with their start and end apart: 17 -> 61, of which waited for: 14 -> 28; matrix products, arithmetic and copies ran while one was open for 13% -> 3% of each run, Pallas kernels for 0% -> 26%
where the time goes in v1:
time: 644 us; the launch traced here: 634 us
  waiting for transfers between devices  250 us (39%)
  Pallas kernels  242 us (38%)
  starting transfers between devices  95 us (15%)
  local copies, waits for them, and re-layouts  36.8 us (6%)
  other arithmetic  9.15 us (1%)
    ppermute x61, waiting for transfers between devices, swap(): return lax.ppermute(x, AXES, [(d, d ^ mask) for d in range(count)])  250 us
    pallas_call x46, Pallas kernels, call(): pl.pallas_call(body, grid_spec=pltpu.PrefetchScalarGridSpec(num_scalar_pr...  242 us
    ppermute x61, starting transfers between devices, swap(): return lax.ppermute(x, AXES, [(d, d ^ mask) for d in range(count)])  95 us
    unnamed x157, local copies, waits for them, and re-layouts  29.9 us
  transfers between devices with their start and end apart: 61, of which 28 were waited for; matrix products, arithmetic and copies ran while one was open for 3% of the time, Pallas kernels for 26%

profile of v1, /device:TPU:0, one launch (start us, length us, event | category | flops | bytes accessed | tf_op | source)
XLA Modules:
  0.0 634.0 jit_solution(13787914386695697789)
XLA Ops:
  3.4 4.0 collective-permute-start.2
  9.3 10.9 %collective-permute-done.2.refs_3_ = bf16[2,64,2048]{2,1,0:T(8,128)(2,1)S(1)} collective-permute-done((bf16[2,64,2048]{2,1,0:T(8,128)(2,1)S(1)}, bf16[2,64,2048]{2,1,0:T(8,128)(2,1)S(1)}, u32[]{:S(2)}, u32[]{:S(2)}) %collective-permute-start.2) | collective-permute-done | bytes 524320 | tf_op jit(solution)/shard_map/ppermute | solution.py:690
  20.2 10.7 %collective-permute-done.1.refs_2_ = bf16[2,64,2048]{2,1,0:T(8,128)(2,1)} collective-permute-done((bf16[2,64,2048]{2,1,0:T(8,128)(2,1)S(1)}, bf16[2,64,2048]{2,1,0:T(8,128)(2,1)}, u32[]{:S(2)}, u32[]{:S(2)}) %collective-permute-start.1) | collective-permute-done | bytes 524320 | tf_op jit(solution)/shard_map/ppermute | solution.py:690
  30.9 3.3 stack.22.refs_0_.refs_1_.refs_8_
  40.6 7.1 %project.1 = (bf16[2,512,128]{2,1,0:T(8,128)(2,1)}, bf16[2,2,4,64,256]{4,3,2,1,0:T(8,128)(2,1)}, f32[2,2,320,256]{3,2,1,0:T(8,128)}) custom-call(s32[5]{0:T(128)} %pad_add_fusion.at_ref, bf16[2,256,2048]{2,1,0:T(8,128)(2,1)} %stack.22.refs_0_.refs_1_.refs_8_, bf16[2,256,2048]{2,1,0:T(8,128)(2,1)} %stack.22.refs_0_.refs_1_.refs_8_, ...), custom_call_target="tpu_custom_call" | custom-call | flops 1610612736 | bytes 8912896 | tf_op jit(solution)/shard_map/project/pallas_call | solution.py:48
  47.8 3.6 collective-permute-start.6
  55.6 14.5 %collective-permute-done.6.refs_5_.refs_7_ = bf16[2,512,128]{2,1,0:T(8,128)(2,1)S(1)} collective-permute-done((bf16[2,512,128]{2,1,0:T(8,128)(2,1)}, bf16[2,512,128]{2,1,0:T(8,128)(2,1)S(1)}, u32[]{:S(2)}, u32[]{:S(2)}) %collective-permute-start.6) | collective-permute-done | bytes 262176 | tf_op jit(solution)/shard_map/ppermute | solution.py:690
  70.2 5.3 collective-permute-done.5.refs_4_.refs_6_
  76.3 13.0 %attend.1 = (bf16[2,256,2048]{2,1,0:T(8,128)(2,1)}, bf16[2,256,2048]{2,1,0:T(8,128)(2,1)}, bf16[2,256,256]{2,1,0:T(8,128)(2,1)}, bf16[2,256,256]{2,1,0:T(8,128)(2,1)}, f32[2,2,4,256]{3,2,1,0:T(4,128)}) custom-call(s32[5]{0:T(128)} %pad_add_fusion.at_ref, bf16[2,64,2048]{2,1,0:T(8,128)(2,1)} %mask.1.refs_0_.refs_1_.refs_6_, ...), custom_call_target="tpu_custom_call" | custom-call | flops 4294967296 | bytes 6291456 | tf_op jit(solution)/shard_map/attend/pallas_call | solution.py:48
  95.0 4.1 chip_sum.4
  101.3 3.8 collective-permute-done.10.refs_4_
  107.7 8.6 %collective-permute-done.9.refs_3_ = bf16[2,64,2048]{2,1,0:T(8,128)(2,1)S(1)} collective-permute-done((bf16[2,64,2048]{2,1,0:T(8,128)(2,1)S(1)}, bf16[2,64,2048]{2,1,0:T(8,128)(2,1)S(1)}, u32[]{:S(2)}, u32[]{:S(2)}) %collective-permute-start.9) | collective-permute-done | bytes 524320 | tf_op jit(solution)/shard_map/ppermute | solution.py:690
  117.2 3.2 stack.23.refs_0_
  120.5 7.0 %collective-permute-done.11.refs_2_ = bf16[2,64,2048]{2,1,0:T(8,128)(2,1)S(1)} collective-permute-done((bf16[2,64,2048]{2,1,0:T(8,128)(2,1)}, bf16[2,64,2048]{2,1,0:T(8,128)(2,1)S(1)}, u32[]{:S(2)}, u32[]{:S(2)}) %collective-permute-start.11) | collective-permute-done | bytes 524320 | tf_op jit(solution)/shard_map/ppermute | solution.py:690
  127.5 10.8 %collective-permute-done.13.refs_4_ = bf16[2,64,2048]{2,1,0:T(8,128)(2,1)S(1)} collective-permute-done((bf16[2,64,2048]{2,1,0:T(8,128)(2,1)}, bf16[2,64,2048]{2,1,0:T(8,128)(2,1)S(1)}, u32[]{:S(2)}, u32[]{:S(2)}) %collective-permute-start.13) | collective-permute-done | bytes 524320 | tf_op jit(solution)/shard_map/ppermute | solution.py:690
  139.1 3.6 middle.1
  146.3 12.5 %collective-permute-done.16.refs_4_ = bf16[2,64,2048]{2,1,0:T(8,128)(2,1)S(1)} collective-permute-done((bf16[2,64,2048]{2,1,0:T(8,128)(2,1)}, bf16[2,64,2048]{2,1,0:T(8,128)(2,1)S(1)}, u32[]{:S(2)}, u32[]{:S(2)}) %collective-permute-start.16) | collective-permute-done | bytes 524320 | tf_op jit(solution)/shard_map/ppermute | solution.py:690
  158.8 9.8 %collective-permute-done.15.refs_3_ = bf16[2,64,2048]{2,1,0:T(8,128)(2,1)S(1)} collective-permute-done((bf16[2,64,2048]{2,1,0:T(8,128)(2,1)}, bf16[2,64,2048]{2,1,0:T(8,128)(2,1)S(1)}, u32[]{:S(2)}, u32[]{:S(2)}) %collective-permute-start.15) | collective-permute-done | bytes 524320 | tf_op jit(solution)/shard_map/ppermute | solution.py:690
  170.2 3.3 stack.24.refs_0_
  173.5 4.3 collective-permute-done.17
  179.2 33.0 %ffn.1 = (bf16[512,2048]{1,0:T(8,128)(2,1)}, bf16[512,2048]{1,0:T(8,128)(2,1)}, bf16[1024,1024]{1,0:T(8,128)(2,1)}, bf16[1024,1024]{1,0:T(8,128)(2,1)}, bf16[1024,1024]{1,0:T(8,128)(2,1)}) custom-call(s32[5]{0:T(128)} %pad_add_fusion.at_ref, bf16[2,256,2048]{2,1,0:T(8,128)(2,1)} %stack.24.refs_0_, bf16[512,2048]{1,0:T(8,128)(2,1)} %bitcast.63, ...), custom_call_target="tpu_custom_call" | custom-call | flops 21474836480 | bytes 39845888 | tf_op jit(solution)/shard_map/ffn/pallas_call | solution.py:48
  212.3 6.7 %grad.24.refs_0_ = bf16[4,256,1024]{2,1,0:T(8,128)(2,1)} custom-call(s32[5]{0:T(128)} %pad_add_fusion.at_ref, bf16[512,2048]{1,0:T(8,128)(2,1)} %get-tuple-element.72.refs_0_, bf16[512,2048]{1,0:T(8,128)(2,1)} %bitcast.86, bf16[512,2048]{1,0:T(8,128)(2,1)} %bitcast.95, bf16[1024,1024]{1,0:T(8,128)(2,1)} %get-tuple-element.73.refs_3_.refs_4_.refs_1_, ...), custom_call_target="tpu_custom_call" | custom-call | flops 2147483648 | bytes 6291456 | tf_op jit(solution)/shard_map/grad/pallas_call | solution.py:48
  220.4 4.0 chip_sum.5
  227.8 6.7 %grad.25.refs_0_ = bf16[4,256,1024]{2,1,0:T(8,128)(2,1)} custom-call(s32[5]{0:T(128)} %pad_add_fusion.at_ref, bf16[2,64,2048]{2,1,0:T(8,128)(2,1)} %get-tuple-element.75.refs_0_.refs_1_, bf16[512,2048]{1,0:T(8,128)(2,1)} %bitcast.64, bf16[512,2048]{1,0:T(8,128)(2,1)} %bitcast.73, bf16[1024,1024]{1,0:T(8,128)(2,1)} %get-tuple-element.76.refs_3_.refs_4_, ...), custom_call_target="tpu_custom_call" | custom-call | flops 2147483648 | bytes 6291456 | tf_op jit(solution)/shard_map/grad/pallas_call | solution.py:48
  234.6 4.2 collective-permute-done.20.refs_2_
  240.0 11.2 %collective-permute-done.22.refs_4_ = bf16[2,64,2048]{2,1,0:T(8,128)(2,1)S(1)} collective-permute-done((bf16[2,64,2048]{2,1,0:T(8,128)(2,1)}, bf16[2,64,2048]{2,1,0:T(8,128)(2,1)S(1)}, u32[]{:S(2)}, u32[]{:S(2)}) %collective-permute-start.22) | collective-permute-done | bytes 524320 | tf_op jit(solution)/shard_map/ppermute | solution.py:690
  252.0 4.0 middle_back.1
  259.5 3.6 collective-permute-start.26
  263.1 10.4 %down.1 = (bf16[512,2048]{1,0:T(8,128)(2,1)}, bf16[512,2048]{1,0:T(8,128)(2,1)}) custom-call(s32[5]{0:T(128)} %pad_add_fusion.at_ref, bf16[2,64,2048]{2,1,0:T(8,128)(2,1)} %get-tuple-element.80.refs_0_.refs_1_, bf16[1024,1024]{1,0:T(8,128)(2,1)} %get-tuple-element.73.refs_3_.refs_4_.refs_1_, bf16[2048,2048]{1,0:T(8,128)(2,1)} %refs_2_.1), custom_call_target="tpu_custom_call" | custom-call | flops 4294967296 | bytes 10485760 | tf_op jit(solution)/shard_map/down/pallas_call | solution.py:48
  273.5 7.2 %collective-permute-done.24.refs_3_ = bf16[2,64,2048]{2,1,0:T(8,128)(2,1)S(1)} collective-permute-done((bf16[2,64,2048]{2,1,0:T(8,128)(2,1)}, bf16[2,64,2048]{2,1,0:T(8,128)(2,1)S(1)}, u32[]{:S(2)}, u32[]{:S(2)}) %collective-permute-start.24) | collective-permute-done | bytes 524320 | tf_op jit(solution)/shard_map/ppermute | solution.py:690
  282.3 3.3 stack.25.refs_0_.refs_1_
  285.5 3.6 collective-permute-start.28
  289.1 20.8 %collective-permute-done.26.refs_5_ = bf16[4,256,1024]{2,1,0:T(8,128)(2,1)S(1)} collective-permute-done((bf16[4,256,1024]{2,1,0:T(8,128)(2,1)}, bf16[4,256,1024]{2,1,0:T(8,128)(2,1)S(1)}, u32[]{:S(2)}, u32[]{:S(2)}) %collective-permute-start.26) | collective-permute-done | bytes 2097184 | tf_op jit(solution)/shard_map/ppermute | solution.py:690
  311.2 5.0 grad.26.refs_0_
  317.5 14.7 %attend_back.1 = (bf16[2,256,256]{2,1,0:T(8,128)(2,1)}, bf16[2,256,256]{2,1,0:T(8,128)(2,1)}, bf16[2,512,128]{2,1,0:T(8,128)(2,1)}, bf16[2,512,128]{2,1,0:T(8,12...) custom-call(s32[5]{0:T(128)} %pad_add_fusion.at_ref, ...), custom_call_target="tpu_custom_call" | custom-call | flops 11811160064 | bytes 7340032 | tf_op jit(solution)/shard_map/attend_back/pallas_call | solution.py:48
  332.2 6.1 collective-permute-start.29
  338.2 18.9 %collective-permute-start.30 = (bf16[2,512,128]{2,1,0:T(8,128)(2,1)}, bf16[2,512,128]{2,1,0:T(8,128)(2,1)S(1)}, u32[]{:S(2)}, u32[]{:S(2)}) collective-permute-start(bf16[2,512,128]{2,1,0:T(8,128)(2,1)} %get-tuple-element.90), channel_id=1, source_target_pairs={{0,16},{1,17},{2,18},{3,19},{4,20},{5,21},{6,22},{7,23},{8,24},{9,... | collective-permute-start | bytes 786440 | tf_op jit(solution)/shard_map/ppermute | solution.py:690
  358.5 4.9 grad.27.refs_0_
  363.4 6.7 %grad.28.refs_0_ = bf16[4,256,1024]{2,1,0:T(8,128)(2,1)} custom-call(s32[5]{0:T(128)} %pad_add_fusion.at_ref, bf16[2,256,1024]{2,1,0:T(8,128)(2,1)} %grad.27.refs_0_, bf16[512,2048]{1,0:T(8,128)(2,1)} %bitcast.66, bf16[512,2048]{1,0:T(8,128)(2,1)} %bitcast.75, bf16[1024,1024]{1,0:T(8,128)(2,1)} %get-tuple-element.87.refs_3_.refs_4_, ...), custom_call_target="tpu_custom_call" | custom-call | flops 2147483648 | bytes 6291456 | tf_op jit(solution)/shard_map/grad/pallas_call | solution.py:48
  371.0 4.7 collective-permute-done.31.refs_4_
  376.4 8.1 %project_back.1 = (bf16[2,256,2048]{2,1,0:T(8,128)(2,1)}, bf16[2,256,2048]{2,1,0:T(8,128)(2,1)}, bf16[2,256,128]{2,1,0:T(8,128)(2,1)}, bf16[2,256,128]{2,1,0:T(8...) custom-call(s32[5]{0:T(128)} %pad_add_fusion.at_ref, bf16[4,256,1024]{2,1,0:T(8,128)(2,1)} %grad.28.refs_0_, ...), custom_call_target="tpu_custom_call" | custom-call | flops 1610612736 | bytes 13107200 | tf_op jit(solution)/shard_map/project_back/pallas_call | solution.py:48
  386.8 8.7 %collective-permute-start.45 = (bf16[2,256,1024]{2,1,0:T(8,128)(2,1)}, bf16[2,256,1024]{2,1,0:T(8,128)(2,1)}, u32[]{:S(2)}, u32[]{:S(2)}) collective-permute-start(bf16[2,256,1024]{2,1,0:T(8,128)(2,1)} %grad.26.refs_0_), channel_id=1, source_target_pairs={{0,16},{1,17},{2,18},{3,19},{4,20},{5,21},{6,22},{7,23},{8,24},{9,... | collective-permute-start | bytes 3145736 | tf_op jit(solution)/shard_map/ppermute | solution.py:690
  395.5 5.1 grad.29.refs_0_
  401.0 4.0 chip_sum.6
  405.0 54.5 %collective-permute-done.45.refs_6_ = bf16[2,256,1024]{2,1,0:T(8,128)(2,1)} collective-permute-done((bf16[2,256,1024]{2,1,0:T(8,128)(2,1)}, bf16[2,256,1024]{2,1,0:T(8,128)(2,1)}, u32[]{:S(2)}, u32[]{:S(2)}) %collective-permute-start.45) | collective-permute-done | bytes 1048608 | tf_op jit(solution)/shard_map/ppermute | solution.py:690
  459.5 4.8 grad.30.refs_0_
  467.5 5.1 grad.31.refs_0_
  478.6 3.6 collective-permute-done.43.refs_2_
  484.3 4.0 chip_sum.7
  488.3 5.0 grad.32.refs_0_
  495.3 3.4 grad.33.refs_0_
  498.7 4.2 grad.34.refs_0_
  503.0 3.4 grad.35.refs_0_
  507.2 3.4 grad.36.refs_0_
  510.6 4.4 grad.37.refs_0_
  521.4 13.3 %collective-permute-done.49.refs_7_ = bf16[1,256,1024]{2,1,0:T(8,128)(2,1)} collective-permute-done((bf16[1,256,1024]{2,1,0:T(8,128)(2,1)S(1)}, bf16[1,256,1024]{2,1,0:T(8,128)(2,1)}, u32[]{:S(2)}, u32[]{:S(2)}) %collective-permute-start.49) | collective-permute-done | bytes 524320 | tf_op jit(solution)/shard_map/ppermute | solution.py:690
  535.0 10.8 %collective-permute-done.50.refs_7_ = bf16[1,256,1024]{2,1,0:T(8,128)(2,1)S(1)} collective-permute-done((bf16[1,256,1024]{2,1,0:T(8,128)(2,1)}, bf16[1,256,1024]{2,1,0:T(8,128)(2,1)S(1)}, u32[]{:S(2)}, u32[]{:S(2)}) %collective-permute-start.50) | collective-permute-done | bytes 524320 | tf_op jit(solution)/shard_map/ppermute | solution.py:690
  549.1 4.9 grad.38.refs_0_
  554.0 5.2 grad.39.refs_0_
  559.3 6.6 %collective-permute-done.51.refs_6_ = bf16[2,256,1024]{2,1,0:T(8,128)(2,1)S(1)} collective-permute-done((bf16[2,256,1024]{2,1,0:T(8,128)(2,1)S(1)}, bf16[2,256,1024]{2,1,0:T(8,128)(2,1)S(1)}, u32[]{:S(2)}, u32[]{:S(2)}) %collective-permute-start.51) | collective-permute-done | bytes 1048608 | tf_op jit(solution)/shard_map/ppermute | solution.py:690
  566.9 4.2 grad.40.refs_0_
  571.1 8.3 %collective-permute-done.52.refs_6_ = bf16[2,256,256]{2,1,0:T(8,128)(2,1)S(1)} collective-permute-done((bf16[2,256,256]{2,1,0:T(8,128)(2,1)S(1)}, bf16[2,256,256]{2,1,0:T(8,128)(2,1)S(1)}, u32[]{:S(2)}, u32[]{:S(2)}) %collective-permute-start.52) | collective-permute-done | bytes 262176 | tf_op jit(solution)/shard_map/ppermute | solution.py:690
  579.5 3.4 collective-permute-start.53
  609.7 4.9 grad.44.refs_0_
  (286 shorter events, 126.3 us)
Async XLA Ops:
  0.6 34.9 %copy-start = (bf16[2048,512]{1,0:T(8,128)(2,1)S(1)}, bf16[2048,512]{1,0:T(8,128)(2,1)}, u32[]{:S(2)}) copy-start(bf16[2048,512]{1,0:T(8,128)(2,1)} %param.17) | copy-start | bytes 6291460
  3.4 16.8 %collective-permute-start.2 = (bf16[2,64,2048]{2,1,0:T(8,128)(2,1)S(1)}, bf16[2,64,2048]{2,1,0:T(8,128)(2,1)S(1)}, u32[]{:S(2)}, u32[]{:S(2)}) collective-permute-start(bf16[2,64,2048]{2,1,0:T(8,128)(2,1)S(1)} %fusion.3.refs_0_), channel_id=1, source_target_pairs={{0,10},{1,11},{2,8},{3,9},{4,14},{5,15},{6,12},{7,13},{8,2},{9,3},... | collective-permute-start | bytes 1572872 | tf_op jit(solution)/shard_map/ppermute | solution.py:690
  7.4 23.5 %collective-permute-start.1 = (bf16[2,64,2048]{2,1,0:T(8,128)(2,1)S(1)}, bf16[2,64,2048]{2,1,0:T(8,128)(2,1)}, u32[]{:S(2)}, u32[]{:S(2)}) collective-permute-start(bf16[2,64,2048]{2,1,0:T(8,128)(2,1)S(1)} %fusion.3.refs_0_), channel_id=1, source_target_pairs={{0,8},{1,9},{2,10},{3,11},{4,12},{5,13},{6,14},{7,15},{8,0},{9,1},... | collective-permute-start | bytes 1572872 | tf_op jit(solution)/shard_map/ppermute | solution.py:690
  7.9 23.0 %collective-permute-start = (bf16[2,64,2048]{2,1,0:T(8,128)(2,1)S(1)}, bf16[2,64,2048]{2,1,0:T(8,128)(2,1)}, u32[]{:S(2)}, u32[]{:S(2)}) collective-permute-start(bf16[2,64,2048]{2,1,0:T(8,128)(2,1)S(1)} %fusion.3.refs_0_), channel_id=1, source_target_pairs={{0,2},{1,3},{2,0},{3,1},{4,6},{5,7},{6,4},{7,5},{8,10},{9,11},{10,... | collective-permute-start | bytes 1572872 | tf_op jit(solution)/shard_map/ppermute | solution.py:690
  34.2 6.5 %collective-permute-start.3 = (bf16[2,256,2048]{2,1,0:T(8,128)(2,1)}, bf16[2,256,2048]{2,1,0:T(8,128)(2,1)}, u32[]{:S(2)}, u32[]{:S(2)}) collective-permute-start(bf16[2,256,2048]{2,1,0:T(8,128)(2,1)} %stack.22.refs_0_.refs_1_.refs_8_), channel_id=1, source_target_pairs={{0,1},{1,0},{2,3},{3,2},{4,5},{5,4},{6,7},{7,6},{8,9},{9,8},{10,11... | collective-permute-start | bytes 6291464 | tf_op jit(solution)/shard_map/ppermute | solution.py:690
  47.8 22.4 %collective-permute-start.6 = (bf16[2,512,128]{2,1,0:T(8,128)(2,1)}, bf16[2,512,128]{2,1,0:T(8,128)(2,1)S(1)}, u32[]{:S(2)}, u32[]{:S(2)}) collective-permute-start(bf16[2,512,128]{2,1,0:T(8,128)(2,1)} %get-tuple-element.62.refs_0_.refs_2_.refs_4_), channel_id=1, source_target_pairs={{0,20},{1,21},{2,22},{3,23},{4,16},{5,17},{6,18},{7,19},{8,28},{9,... | collective-permute-start | bytes 786440 | tf_op jit(solution)/shard_map/ppermute | solution.py:690
  51.4 24.1 %collective-permute-start.5 = (bf16[2,512,128]{2,1,0:T(8,128)(2,1)}, bf16[2,512,128]{2,1,0:T(8,128)(2,1)S(1)}, u32[]{:S(2)}, u32[]{:S(2)}) collective-permute-start(bf16[2,512,128]{2,1,0:T(8,128)(2,1)} %get-tuple-element.62.refs_0_.refs_2_.refs_4_), channel_id=1, source_target_pairs={{0,16},{1,17},{2,18},{3,19},{4,20},{5,21},{6,22},{7,23},{8,24},{9,... | collective-permute-start | bytes 786440 | tf_op jit(solution)/shard_map/ppermute | solution.py:690
  51.7 23.8 %collective-permute-start.4 = (bf16[2,512,128]{2,1,0:T(8,128)(2,1)}, bf16[2,512,128]{2,1,0:T(8,128)(2,1)S(1)}, u32[]{:S(2)}, u32[]{:S(2)}) collective-permute-start(bf16[2,512,128]{2,1,0:T(8,128)(2,1)} %get-tuple-element.62.refs_0_.refs_2_.refs_4_), channel_id=1, source_target_pairs={{0,4},{1,5},{2,6},{3,7},{4,0},{5,1},{6,2},{7,3},{8,12},{9,13},{10,... | collective-permute-start | bytes 786440 | tf_op jit(solution)/shard_map/ppermute | solution.py:690
  89.3 4.4 collective-permute-start.7
  89.4 15.7 %collective-permute-start.10 = (bf16[2,64,2048]{2,1,0:T(8,128)(2,1)S(1)}, bf16[2,64,2048]{2,1,0:T(8,128)(2,1)S(1)}, u32[]{:S(2)}, u32[]{:S(2)}) collective-permute-start(bf16[2,64,2048]{2,1,0:T(8,128)(2,1)S(1)} %copy-done.12), channel_id=1, source_target_pairs={{0,10},{1,11},{2,8},{3,9},{4,14},{5,15},{6,12},{7,13},{8,2},{9,3},... | collective-permute-start | bytes 1572872 | tf_op jit(solution)/shard_map/ppermute | solution.py:690
  91.0 25.2 %collective-permute-start.9 = (bf16[2,64,2048]{2,1,0:T(8,128)(2,1)S(1)}, bf16[2,64,2048]{2,1,0:T(8,128)(2,1)S(1)}, u32[]{:S(2)}, u32[]{:S(2)}) collective-permute-start(bf16[2,64,2048]{2,1,0:T(8,128)(2,1)S(1)} %copy-done.12), channel_id=1, source_target_pairs={{0,8},{1,9},{2,10},{3,11},{4,12},{5,13},{6,14},{7,15},{8,0},{9,1},... | collective-permute-start | bytes 1572872 | tf_op jit(solution)/shard_map/ppermute | solution.py:690
  92.3 24.0 %collective-permute-start.8 = (bf16[2,64,2048]{2,1,0:T(8,128)(2,1)S(1)}, bf16[2,64,2048]{2,1,0:T(8,128)(2,1)S(1)}, u32[]{:S(2)}, u32[]{:S(2)}) collective-permute-start(bf16[2,64,2048]{2,1,0:T(8,128)(2,1)S(1)} %copy-done.12), channel_id=1, source_target_pairs={{0,2},{1,3},{2,0},{3,1},{4,6},{5,7},{6,4},{7,5},{8,10},{9,11},{10,... | collective-permute-start | bytes 1572872 | tf_op jit(solution)/shard_map/ppermute | solution.py:690
  99.1 28.3 %collective-permute-start.11 = (bf16[2,64,2048]{2,1,0:T(8,128)(2,1)}, bf16[2,64,2048]{2,1,0:T(8,128)(2,1)S(1)}, u32[]{:S(2)}, u32[]{:S(2)}) collective-permute-start(bf16[2,64,2048]{2,1,0:T(8,128)(2,1)} %get-tuple-element.67), channel_id=1, source_target_pairs={{0,2},{1,3},{2,0},{3,1},{4,6},{5,7},{6,4},{7,5},{8,10},{9,11},{10,... | collective-permute-start | bytes 1572872 | tf_op jit(solution)/shard_map/ppermute | solution.py:690
  100.5 27.0 %collective-permute-start.12 = (bf16[2,64,2048]{2,1,0:T(8,128)(2,1)}, bf16[2,64,2048]{2,1,0:T(8,128)(2,1)S(1)}, u32[]{:S(2)}, u32[]{:S(2)}) collective-permute-start(bf16[2,64,2048]{2,1,0:T(8,128)(2,1)} %get-tuple-element.68), channel_id=1, source_target_pairs={{0,8},{1,9},{2,10},{3,11},{4,12},{5,13},{6,14},{7,15},{8,0},{9,1},... | collective-permute-start | bytes 1572872 | tf_op jit(solution)/shard_map/ppermute | solution.py:690
  105.1 33.2 %collective-permute-start.13 = (bf16[2,64,2048]{2,1,0:T(8,128)(2,1)}, bf16[2,64,2048]{2,1,0:T(8,128)(2,1)S(1)}, u32[]{:S(2)}, u32[]{:S(2)}) collective-permute-start(bf16[2,64,2048]{2,1,0:T(8,128)(2,1)} %get-tuple-element.69), channel_id=1, source_target_pairs={{0,10},{1,11},{2,8},{3,9},{4,14},{5,15},{6,12},{7,13},{8,2},{9,3},... | collective-permute-start | bytes 1572872 | tf_op jit(solution)/shard_map/ppermute | solution.py:690
  142.8 16.0 %collective-permute-start.16 = (bf16[2,64,2048]{2,1,0:T(8,128)(2,1)}, bf16[2,64,2048]{2,1,0:T(8,128)(2,1)S(1)}, u32[]{:S(2)}, u32[]{:S(2)}) collective-permute-start(bf16[2,64,2048]{2,1,0:T(8,128)(2,1)} %get-tuple-element.71.refs_0_.refs_1_), channel_id=1, source_target_pairs={{0,10},{1,11},{2,8},{3,9},{4,14},{5,15},{6,12},{7,13},{8,2},{9,3},... | collective-permute-start | bytes 1572872 | tf_op jit(solution)/shard_map/ppermute | solution.py:690
  144.4 24.2 %collective-permute-start.15 = (bf16[2,64,2048]{2,1,0:T(8,128)(2,1)}, bf16[2,64,2048]{2,1,0:T(8,128)(2,1)S(1)}, u32[]{:S(2)}, u32[]{:S(2)}) collective-permute-start(bf16[2,64,2048]{2,1,0:T(8,128)(2,1)} %get-tuple-element.71.refs_0_.refs_1_), channel_id=1, source_target_pairs={{0,8},{1,9},{2,10},{3,11},{4,12},{5,13},{6,14},{7,15},{8,0},{9,1},... | collective-permute-start | bytes 1572872 | tf_op jit(solution)/shard_map/ppermute | solution.py:690
  145.7 23.0 %collective-permute-start.14 = (bf16[2,64,2048]{2,1,0:T(8,128)(2,1)}, bf16[2,64,2048]{2,1,0:T(8,128)(2,1)S(1)}, u32[]{:S(2)}, u32[]{:S(2)}) collective-permute-start(bf16[2,64,2048]{2,1,0:T(8,128)(2,1)} %get-tuple-element.71.refs_0_.refs_1_), channel_id=1, source_target_pairs={{0,2},{1,3},{2,0},{3,1},{4,6},{5,7},{6,4},{7,5},{8,10},{9,11},{10,... | collective-permute-start | bytes 1572872 | tf_op jit(solution)/shard_map/ppermute | solution.py:690
  146.3 27.2 %collective-permute-start.18 = (bf16[2,256,2048]{2,1,0:T(8,128)(2,1)S(1)}, bf16[2,256,2048]{2,1,0:T(8,128)(2,1)S(1)}, u32[]{:S(2)}, u32[]{:S(2)}) collective-permute-start(bf16[2,256,2048]{2,1,0:T(8,128)(2,1)S(1)} %copy-done.3), channel_id=1, source_target_pairs={{0,1},{1,0},{2,3},{3,2},{4,5},{5,4},{6,7},{7,6},{8,9},{9,8},{10,11... | collective-permute-start | bytes 6291464 | tf_op jit(solution)/shard_map/ppermute | solution.py:690
  173.5 4.4 collective-permute-start.17
  212.1 6.9 %collective-permute-start.19 = (bf16[512,2048]{1,0:T(8,128)(2,1)}, bf16[512,2048]{1,0:T(8,128)(2,1)S(1)}, u32[]{:S(2)}, u32[]{:S(2)}) collective-permute-start(bf16[512,2048]{1,0:T(8,128)(2,1)} %get-tuple-element.72.refs_0_), channel_id=1, source_target_pairs={{0,1},{1,0},{2,3},{3,2},{4,5},{5,4},{6,7},{7,6},{8,9},{9,8},{10,11... | collective-permute-start | bytes 6291464 | tf_op jit(solution)/shard_map/ppermute | solution.py:690
  224.3 14.4 %collective-permute-start.20 = (bf16[2,64,2048]{2,1,0:T(8,128)(2,1)}, bf16[2,64,2048]{2,1,0:T(8,128)(2,1)S(1)}, u32[]{:S(2)}, u32[]{:S(2)}) collective-permute-start(bf16[2,64,2048]{2,1,0:T(8,128)(2,1)} %get-tuple-element.77), channel_id=1, source_target_pairs={{0,2},{1,3},{2,0},{3,1},{4,6},{5,7},{6,4},{7,5},{8,10},{9,11},{10,... | collective-permute-start | bytes 1572872 | tf_op jit(solution)/shard_map/ppermute | solution.py:690
  225.0 15.0 %collective-permute-start.21 = (bf16[2,64,2048]{2,1,0:T(8,128)(2,1)}, bf16[2,64,2048]{2,1,0:T(8,128)(2,1)S(1)}, u32[]{:S(2)}, u32[]{:S(2)}) collective-permute-start(bf16[2,64,2048]{2,1,0:T(8,128)(2,1)} %get-tuple-element.78), channel_id=1, source_target_pairs={{0,8},{1,9},{2,10},{3,11},{4,12},{5,13},{6,14},{7,15},{8,0},{9,1},... | collective-permute-start | bytes 1572872 | tf_op jit(solution)/shard_map/ppermute | solution.py:690
  225.8 25.4 %collective-permute-start.22 = (bf16[2,64,2048]{2,1,0:T(8,128)(2,1)}, bf16[2,64,2048]{2,1,0:T(8,128)(2,1)S(1)}, u32[]{:S(2)}, u32[]{:S(2)}) collective-permute-start(bf16[2,64,2048]{2,1,0:T(8,128)(2,1)} %get-tuple-element.79), channel_id=1, source_target_pairs={{0,10},{1,11},{2,8},{3,9},{4,14},{5,15},{6,12},{7,13},{8,2},{9,3},... | collective-permute-start | bytes 1572872 | tf_op jit(solution)/shard_map/ppermute | solution.py:690
  256.0 17.5 %collective-permute-start.25 = (bf16[2,64,2048]{2,1,0:T(8,128)(2,1)}, bf16[2,64,2048]{2,1,0:T(8,128)(2,1)S(1)}, u32[]{:S(2)}, u32[]{:S(2)}) collective-permute-start(bf16[2,64,2048]{2,1,0:T(8,128)(2,1)} %get-tuple-element.80.refs_0_.refs_1_), channel_id=1, source_target_pairs={{0,10},{1,11},{2,8},{3,9},{4,14},{5,15},{6,12},{7,13},{8,2},{9,3},... | collective-permute-start | bytes 1572872 | tf_op jit(solution)/shard_map/ppermute | solution.py:690
  256.9 23.8 %collective-permute-start.24 = (bf16[2,64,2048]{2,1,0:T(8,128)(2,1)}, bf16[2,64,2048]{2,1,0:T(8,128)(2,1)S(1)}, u32[]{:S(2)}, u32[]{:S(2)}) collective-permute-start(bf16[2,64,2048]{2,1,0:T(8,128)(2,1)} %get-tuple-element.80.refs_0_.refs_1_), channel_id=1, source_target_pairs={{0,8},{1,9},{2,10},{3,11},{4,12},{5,13},{6,14},{7,15},{8,0},{9,1},... | collective-permute-start | bytes 1572872 | tf_op jit(solution)/shard_map/ppermute | solution.py:690
  258.2 23.3 %collective-permute-start.23 = (bf16[2,64,2048]{2,1,0:T(8,128)(2,1)}, bf16[2,64,2048]{2,1,0:T(8,128)(2,1)S(1)}, u32[]{:S(2)}, u32[]{:S(2)}) collective-permute-start(bf16[2,64,2048]{2,1,0:T(8,128)(2,1)} %get-tuple-element.80.refs_0_.refs_1_), channel_id=1, source_target_pairs={{0,2},{1,3},{2,0},{3,1},{4,6},{5,7},{6,4},{7,5},{8,10},{9,11},{10,... | collective-permute-start | bytes 1572872 | tf_op jit(solution)/shard_map/ppermute | solution.py:690
  259.5 50.3 %collective-permute-start.26 = (bf16[4,256,1024]{2,1,0:T(8,128)(2,1)}, bf16[4,256,1024]{2,1,0:T(8,128)(2,1)S(1)}, u32[]{:S(2)}, u32[]{:S(2)}) collective-permute-start(bf16[4,256,1024]{2,1,0:T(8,128)(2,1)} %grad.24.refs_0_), channel_id=1, source_target_pairs={{0,4},{1,5},{2,6},{3,7},{4,0},{5,1},{6,2},{7,3},{8,12},{9,13},{10,... | collective-permute-start | bytes 6291464 | tf_op jit(solution)/shard_map/ppermute | solution.py:690
  285.5 30.7 %collective-permute-start.27 = (bf16[2,256,2048]{2,1,0:T(8,128)(2,1)}, bf16[2,256,2048]{2,1,0:T(8,128)(2,1)S(1)}, u32[]{:S(2)}, u32[]{:S(2)}) collective-permute-start(bf16[2,256,2048]{2,1,0:T(8,128)(2,1)} %stack.25.refs_0_.refs_1_), channel_id=1, source_target_pairs={{0,1},{1,0},{2,3},{3,2},{4,5},{5,4},{6,7},{7,6},{8,9},{9,8},{10,11... | collective-permute-start | bytes 6291464 | tf_op jit(solution)/shard_map/ppermute | solution.py:690
  285.5 71.6 %collective-permute-start.28 = (bf16[4,256,1024]{2,1,0:T(8,128)(2,1)}, bf16[4,256,1024]{2,1,0:T(8,128)(2,1)S(1)}, u32[]{:S(2)}, u32[]{:S(2)}) collective-permute-start(bf16[4,256,1024]{2,1,0:T(8,128)(2,1)} %grad.25.refs_0_), channel_id=1, source_target_pairs={{0,4},{1,5},{2,6},{3,7},{4,0},{5,1},{6,2},{7,3},{8,12},{9,13},{10,... | collective-permute-start | bytes 6291464 | tf_op jit(solution)/shard_map/ppermute | solution.py:690
  332.2 38.0 %collective-permute-start.29 = (bf16[2,512,128]{2,1,0:T(8,128)(2,1)}, bf16[2,512,128]{2,1,0:T(8,128)(2,1)S(1)}, u32[]{:S(2)}, u32[]{:S(2)}) collective-permute-start(bf16[2,512,128]{2,1,0:T(8,128)(2,1)} %get-tuple-element.89), channel_id=1, source_target_pairs={{0,4},{1,5},{2,6},{3,7},{4,0},{5,1},{6,2},{7,3},{8,12},{9,13},{10,... | collective-permute-start | bytes 786440 | tf_op jit(solution)/shard_map/ppermute | solution.py:690
  338.2 32.8 %collective-permute-start.30 = (bf16[2,512,128]{2,1,0:T(8,128)(2,1)}, bf16[2,512,128]{2,1,0:T(8,128)(2,1)S(1)}, u32[]{:S(2)}, u32[]{:S(2)}) collective-permute-start(bf16[2,512,128]{2,1,0:T(8,128)(2,1)} %get-tuple-element.90), channel_id=1, source_target_pairs={{0,16},{1,17},{2,18},{3,19},{4,20},{5,21},{6,22},{7,23},{8,24},{9,... | collective-permute-start | bytes 786440 | tf_op jit(solution)/shard_map/ppermute | solution.py:690
  357.1 18.5 %collective-permute-start.31 = (bf16[2,512,128]{2,1,0:T(8,128)(2,1)}, bf16[2,512,128]{2,1,0:T(8,128)(2,1)S(1)}, u32[]{:S(2)}, u32[]{:S(2)}) collective-permute-start(bf16[2,512,128]{2,1,0:T(8,128)(2,1)} %get-tuple-element.91), channel_id=1, source_target_pairs={{0,20},{1,21},{2,22},{3,23},{4,16},{5,17},{6,18},{7,19},{8,28},{9,... | collective-permute-start | bytes 786440 | tf_op jit(solution)/shard_map/ppermute | solution.py:690
  384.5 16.1 %collective-permute-start.32 = (bf16[2,256,2048]{2,1,0:T(8,128)(2,1)}, bf16[2,256,2048]{2,1,0:T(8,128)(2,1)}, u32[]{:S(2)}, u32[]{:S(2)}) collective-permute-start(bf16[2,256,2048]{2,1,0:T(8,128)(2,1)} %get-tuple-element.93.refs_0_), channel_id=1, source_target_pairs={{0,1},{1,0},{2,3},{3,2},{4,5},{5,4},{6,7},{7,6},{8,9},{9,8},{10,11... | collective-permute-start | bytes 6291464 | tf_op jit(solution)/shard_map/ppermute | solution.py:690
  384.6 82.3 %collective-permute-start.35 = (bf16[512,2048]{1,0:T(8,128)(2,1)}, bf16[512,2048]{1,0:T(8,128)(2,1)}, u32[]{:S(2)}, u32[]{:S(2)}) collective-permute-start(bf16[512,2048]{1,0:T(8,128)(2,1)} %get-tuple-element.81.refs_0_), channel_id=1, source_target_pairs={{0,1},{1,0},{2,3},{3,2},{4,5},{5,4},{6,7},{7,6},{8,9},{9,8},{10,11... | collective-permute-start | bytes 6291464 | tf_op jit(solution)/shard_map/ppermute | solution.py:690
  385.1 92.1 %collective-permute-start.42 = (bf16[4,256,1024]{2,1,0:T(8,128)(2,1)}, bf16[4,256,1024]{2,1,0:T(8,128)(2,1)S(1)}, u32[]{:S(2)}, u32[]{:S(2)}) collective-permute-start(bf16[4,256,1024]{2,1,0:T(8,128)(2,1)} %grad.28.refs_0_), channel_id=1, source_target_pairs={{0,4},{1,5},{2,6},{3,7},{4,0},{5,1},{6,2},{7,3},{8,12},{9,13},{10,... | collective-permute-start | bytes 6291464 | tf_op jit(solution)/shard_map/ppermute | solution.py:690
  386.8 72.7 %collective-permute-start.45 = (bf16[2,256,1024]{2,1,0:T(8,128)(2,1)}, bf16[2,256,1024]{2,1,0:T(8,128)(2,1)}, u32[]{:S(2)}, u32[]{:S(2)}) collective-permute-start(bf16[2,256,1024]{2,1,0:T(8,128)(2,1)} %grad.26.refs_0_), channel_id=1, source_target_pairs={{0,16},{1,17},{2,18},{3,19},{4,20},{5,21},{6,22},{7,23},{8,24},{9,... | collective-permute-start | bytes 3145736 | tf_op jit(solution)/shard_map/ppermute | solution.py:690
  395.5 115.1 %collective-permute-start.48 = (bf16[2,256,1024]{2,1,0:T(8,128)(2,1)}, bf16[2,256,1024]{2,1,0:T(8,128)(2,1)}, u32[]{:S(2)}, u32[]{:S(2)}) collective-permute-start(bf16[2,256,1024]{2,1,0:T(8,128)(2,1)} %grad.27.refs_0_), channel_id=1, source_target_pairs={{0,16},{1,17},{2,18},{3,19},{4,20},{5,21},{6,22},{7,23},{8,24},{9,... | collective-permute-start | bytes 3145736 | tf_op jit(solution)/shard_map/ppermute | solution.py:690
  400.6 75.6 %collective-permute-start.44 = (bf16[4,256,256]{2,1,0:T(8,128)(2,1)}, bf16[4,256,256]{2,1,0:T(8,128)(2,1)S(1)}, u32[]{:S(2)}, u32[]{:S(2)}) collective-permute-start(bf16[4,256,256]{2,1,0:T(8,128)(2,1)} %grad.29.refs_0_), channel_id=1, source_target_pairs={{0,4},{1,5},{2,6},{3,7},{4,0},{5,1},{6,2},{7,3},{8,12},{9,13},{10,... | collective-permute-start | bytes 1572872 | tf_op jit(solution)/shard_map/ppermute | solution.py:690
  401.0 58.5 %copy-start.57 = (f32[4224]{0:T(1024)}, f32[4224]{0:T(1024)S(1)}, u32[]{:S(2)}) copy-start(f32[4224]{0:T(1024)S(1)} %concatenate.15) | copy-start | bytes 50692
  459.5 4.8 collective-permute-start.33
  464.3 17.9 %collective-permute-start.46 = (bf16[4,256,128]{2,1,0:T(8,128)(2,1)}, bf16[4,256,128]{2,1,0:T(8,128)(2,1)S(1)}, u32[]{:S(2)}, u32[]{:S(2)}) collective-permute-start(bf16[4,256,128]{2,1,0:T(8,128)(2,1)} %grad.30.refs_0_), channel_id=1, source_target_pairs={{0,4},{1,5},{2,6},{3,7},{4,0},{5,1},{6,2},{7,3},{8,12},{9,13},{10,... | collective-permute-start | bytes 786440 | tf_op jit(solution)/shard_map/ppermute | solution.py:690
  466.9 5.7 collective-permute-start.34
  472.6 33.7 %collective-permute-start.47 = (bf16[4,256,256]{2,1,0:T(8,128)(2,1)}, bf16[4,256,256]{2,1,0:T(8,128)(2,1)S(1)}, u32[]{:S(2)}, u32[]{:S(2)}) collective-permute-start(bf16[4,256,256]{2,1,0:T(8,128)(2,1)} %grad.31.refs_0_), channel_id=1, source_target_pairs={{0,4},{1,5},{2,6},{3,7},{4,0},{5,1},{6,2},{7,3},{8,12},{9,13},{10,... | collective-permute-start | bytes 1572872 | tf_op jit(solution)/shard_map/ppermute | solution.py:690
  476.2 6.0 collective-permute-start.43
  477.2 39.1 %collective-permute-start.39 = (bf16[2,64,2048]{2,1,0:T(8,128)(2,1)}, bf16[2,64,2048]{2,1,0:T(8,128)(2,1)S(1)}, u32[]{:S(2)}, u32[]{:S(2)}) collective-permute-start(bf16[2,64,2048]{2,1,0:T(8,128)(2,1)} %get-tuple-element.108), channel_id=1, source_target_pairs={{0,2},{1,3},{2,0},{3,1},{4,6},{5,7},{6,4},{7,5},{8,10},{9,11},{10,... | collective-permute-start | bytes 1572872 | tf_op jit(solution)/shard_map/ppermute | solution.py:690
  482.2 36.0 %collective-permute-start.40 = (bf16[2,64,2048]{2,1,0:T(8,128)(2,1)S(1)}, bf16[2,64,2048]{2,1,0:T(8,128)(2,1)S(1)}, u32[]{:S(2)}, u32[]{:S(2)}) collective-permute-start(bf16[2,64,2048]{2,1,0:T(8,128)(2,1)S(1)} %copy-done.70), channel_id=1, source_target_pairs={{0,8},{1,9},{2,10},{3,11},{4,12},{5,13},{6,14},{7,15},{8,0},{9,1},... | collective-permute-start | bytes 1572872 | tf_op jit(solution)/shard_map/ppermute | solution.py:690
  482.2 37.4 %collective-permute-start.41 = (bf16[2,64,2048]{2,1,0:T(8,128)(2,1)}, bf16[2,64,2048]{2,1,0:T(8,128)(2,1)S(1)}, u32[]{:S(2)}, u32[]{:S(2)}) collective-permute-start(bf16[2,64,2048]{2,1,0:T(8,128)(2,1)} %get-tuple-element.110), channel_id=1, source_target_pairs={{0,10},{1,11},{2,8},{3,9},{4,14},{5,15},{6,12},{7,13},{8,2},{9,3},... | collective-permute-start | bytes 1572872 | tf_op jit(solution)/shard_map/ppermute | solution.py:690
  506.4 28.4 %collective-permute-start.49 = (bf16[1,256,1024]{2,1,0:T(8,128)(2,1)S(1)}, bf16[1,256,1024]{2,1,0:T(8,128)(2,1)}, u32[]{:S(2)}, u32[]{:S(2)}) collective-permute-start(bf16[1,256,1024]{2,1,0:T(8,128)(2,1)S(1)} %copy-done.23), channel_id=1, source_target_pairs={{0,8},{1,9},{2,10},{3,11},{4,12},{5,13},{6,14},{7,15},{8,0},{9,1},... | collective-permute-start | bytes 1572872 | tf_op jit(solution)/shard_map/ppermute | solution.py:690
  515.0 31.7 %copy-start.28 = (f32[2,64,2048]{2,1,0:T(8,128)S(1)}, f32[2,64,2048]{2,1,0:T(8,128)}, u32[]{:S(2)}) copy-start(f32[2,64,2048]{2,1,0:T(8,128)} %get-tuple-element.107) | copy-start | bytes 3145732
  515.0 30.9 %collective-permute-start.50 = (bf16[1,256,1024]{2,1,0:T(8,128)(2,1)}, bf16[1,256,1024]{2,1,0:T(8,128)(2,1)S(1)}, u32[]{:S(2)}, u32[]{:S(2)}) collective-permute-start(bf16[1,256,1024]{2,1,0:T(8,128)(2,1)} %grad.37.refs_0_), channel_id=1, source_target_pairs={{0,8},{1,9},{2,10},{3,11},{4,12},{5,13},{6,14},{7,15},{8,0},{9,1},... | collective-permute-start | bytes 1572872 | tf_op jit(solution)/shard_map/ppermute | solution.py:690
  516.3 49.6 %collective-permute-start.51 = (bf16[2,256,1024]{2,1,0:T(8,128)(2,1)S(1)}, bf16[2,256,1024]{2,1,0:T(8,128)(2,1)S(1)}, u32[]{:S(2)}, u32[]{:S(2)}) collective-permute-start(bf16[2,256,1024]{2,1,0:T(8,128)(2,1)S(1)} %copy-done.14), channel_id=1, source_target_pairs={{0,16},{1,17},{2,18},{3,19},{4,20},{5,21},{6,22},{7,23},{8,24},{9,... | collective-permute-start | bytes 3145736 | tf_op jit(solution)/shard_map/ppermute | solution.py:690
  518.2 67.6 %collective-permute-start.36 = (bf16[2,64,2048]{2,1,0:T(8,128)(2,1)}, bf16[2,64,2048]{2,1,0:T(8,128)(2,1)S(1)}, u32[]{:S(2)}, u32[]{:S(2)}) collective-permute-start(bf16[2,64,2048]{2,1,0:T(8,128)(2,1)} %get-tuple-element.104), channel_id=1, source_target_pairs={{0,2},{1,3},{2,0},{3,1},{4,6},{5,7},{6,4},{7,5},{8,10},{9,11},{10,... | collective-permute-start | bytes 1572872 | tf_op jit(solution)/shard_map/ppermute | solution.py:690
  519.6 67.0 %collective-permute-start.37 = (bf16[2,64,2048]{2,1,0:T(8,128)(2,1)}, bf16[2,64,2048]{2,1,0:T(8,128)(2,1)S(1)}, u32[]{:S(2)}, u32[]{:S(2)}) collective-permute-start(bf16[2,64,2048]{2,1,0:T(8,128)(2,1)} %get-tuple-element.105), channel_id=1, source_target_pairs={{0,8},{1,9},{2,10},{3,11},{4,12},{5,13},{6,14},{7,15},{8,0},{9,1},... | collective-permute-start | bytes 1572872 | tf_op jit(solution)/shard_map/ppermute | solution.py:690
  534.7 54.3 %collective-permute-start.38 = (bf16[2,64,2048]{2,1,0:T(8,128)(2,1)}, bf16[2,64,2048]{2,1,0:T(8,128)(2,1)}, u32[]{:S(2)}, u32[]{:S(2)}) collective-permute-start(bf16[2,64,2048]{2,1,0:T(8,128)(2,1)} %get-tuple-element.106), channel_id=1, source_target_pairs={{0,10},{1,11},{2,8},{3,9},{4,14},{5,15},{6,12},{7,13},{8,2},{9,3},... | collective-permute-start | bytes 1572872 | tf_op jit(solution)/shard_map/ppermute | solution.py:690
  545.9 33.6 %collective-permute-start.52 = (bf16[2,256,256]{2,1,0:T(8,128)(2,1)S(1)}, bf16[2,256,256]{2,1,0:T(8,128)(2,1)S(1)}, u32[]{:S(2)}, u32[]{:S(2)}) collective-permute-start(bf16[2,256,256]{2,1,0:T(8,128)(2,1)S(1)} %copy-done.27), channel_id=1, source_target_pairs={{0,16},{1,17},{2,18},{3,19},{4,20},{5,21},{6,22},{7,23},{8,24},{9,... | collective-permute-start | bytes 786440 | tf_op jit(solution)/shard_map/ppermute | solution.py:690
  565.8 37.8 %collective-permute-start.55 = (f32[33,128]{1,0:T(8,128)S(1)}, f32[33,128]{1,0:T(8,128)S(1)}, u32[]{:S(2)}, u32[]{:S(2)}) collective-permute-start(f32[33,128]{1,0:T(8,128)S(1)} %copy-done.53), channel_id=1, source_target_pairs={{0,4},{1,5},{2,6},{3,7},{4,0},{5,1},{6,2},{7,3},{8,12},{9,13},{10,... | collective-permute-start | bytes 50696 | tf_op jit(solution)/shard_map/ppermute | solution.py:690
  579.5 12.6 %collective-permute-start.53 = (bf16[2,256,128]{2,1,0:T(8,128)(2,1)S(1)}, bf16[2,256,128]{2,1,0:T(8,128)(2,1)S(1)}, u32[]{:S(2)}, u32[]{:S(2)}) collective-permute-start(bf16[2,256,128]{2,1,0:T(8,128)(2,1)S(1)} %copy-done.46), channel_id=1, source_target_pairs={{0,16},{1,17},{2,18},{3,19},{4,20},{5,21},{6,22},{7,23},{8,24},{9,... | collective-permute-start | bytes 393224 | tf_op jit(solution)/shard_map/ppermute | solution.py:690
  585.8 14.1 %collective-permute-start.54 = (bf16[2,256,256]{2,1,0:T(8,128)(2,1)S(1)}, bf16[2,256,256]{2,1,0:T(8,128)(2,1)S(1)}, u32[]{:S(2)}, u32[]{:S(2)}) collective-permute-start(bf16[2,256,256]{2,1,0:T(8,128)(2,1)S(1)} %copy-done.24), channel_id=1, source_target_pairs={{0,16},{1,17},{2,18},{3,19},{4,20},{5,21},{6,22},{7,23},{8,24},{9,... | collective-permute-start | bytes 786440 | tf_op jit(solution)/shard_map/ppermute | solution.py:690
  586.5 22.4 %collective-permute-start.56 = (bf16[1,256,1024]{2,1,0:T(8,128)(2,1)S(1)}, bf16[1,256,1024]{2,1,0:T(8,128)(2,1)S(1)}, u32[]{:S(2)}, u32[]{:S(2)}) collective-permute-start(bf16[1,256,1024]{2,1,0:T(8,128)(2,1)S(1)} %copy-done.22), channel_id=1, source_target_pairs={{0,8},{1,9},{2,10},{3,11},{4,12},{5,13},{6,14},{7,15},{8,0},{9,1},... | collective-permute-start | bytes 1572872 | tf_op jit(solution)/shard_map/ppermute | solution.py:690
  589.0 25.6 %collective-permute-start.57 = (bf16[1,256,256]{2,1,0:T(8,128)(2,1)}, bf16[1,256,256]{2,1,0:T(8,128)(2,1)S(1)}, u32[]{:S(2)}, u32[]{:S(2)}) collective-permute-start(bf16[1,256,256]{2,1,0:T(8,128)(2,1)} %grad.41.refs_0_), channel_id=1, source_target_pairs={{0,8},{1,9},{2,10},{3,11},{4,12},{5,13},{6,14},{7,15},{8,0},{9,1},... | collective-permute-start | bytes 393224 | tf_op jit(solution)/shard_map/ppermute | solution.py:690
  595.5 23.0 %collective-permute-start.58 = (bf16[1,256,128]{2,1,0:T(8,128)(2,1)}, bf16[1,256,128]{2,1,0:T(8,128)(2,1)S(1)}, u32[]{:S(2)}, u32[]{:S(2)}) collective-permute-start(bf16[1,256,128]{2,1,0:T(8,128)(2,1)} %grad.42.refs_0_), channel_id=1, source_target_pairs={{0,8},{1,9},{2,10},{3,11},{4,12},{5,13},{6,14},{7,15},{8,0},{9,1},... | collective-permute-start | bytes 196616 | tf_op jit(solution)/shard_map/ppermute | solution.py:690
  603.6 21.1 %collective-permute-start.59 = (bf16[1,256,256]{2,1,0:T(8,128)(2,1)}, bf16[1,256,256]{2,1,0:T(8,128)(2,1)S(1)}, u32[]{:S(2)}, u32[]{:S(2)}) collective-permute-start(bf16[1,256,256]{2,1,0:T(8,128)(2,1)} %grad.43.refs_0_), channel_id=1, source_target_pairs={{0,8},{1,9},{2,10},{3,11},{4,12},{5,13},{6,14},{7,15},{8,0},{9,1},... | collective-permute-start | bytes 393224 | tf_op jit(solution)/shard_map/ppermute | solution.py:690
  606.2 22.3 %collective-permute-start.60 = (f32[33,128]{1,0:T(8,128)}, f32[33,128]{1,0:T(8,128)S(1)}, u32[]{:S(2)}, u32[]{:S(2)}) collective-permute-start(f32[33,128]{1,0:T(8,128)} %add.215.refs_0_.refs_1_), channel_id=1, source_target_pairs={{0,16},{1,17},{2,18},{3,19},{4,20},{5,21},{6,22},{7,23},{8,24},{9,... | collective-permute-start | bytes 50696 | tf_op jit(solution)/shard_map/ppermute | solution.py:690
  (71 other events, 491.5 us)
